TPU v7x, 128 devices: a whole 4x4x4 slice. The times are simulated.
128 devices in a mesh: row: 8 (over x_lo, y), col: 16 (over z, x_hi, core).
Axes of the slice: x: 4 (x_hi: 2, x_lo: 2; x = x_hi * 2 + x_lo), y: 4, z: 4, core: 2. Of those that a mesh axis runs over, the one named last changes fastest.
Arguments:
- pair: float32 [256, 256, 128], P('row', 'col'), may hold values from -6 to 6
- cotangent: float32 [256, 256, 128], P('row', 'col'), may hold values from -6 to 6
- tri_bias: float32 [4, 256, 256], P(None, 'col'), may hold values from -4 to 400
- valid_length: int32 [1], replicated, may hold values from 128 to 256
- gain_first: float32 [128], replicated, may hold values from 0.25 to 1.75
- w_first: float32 [128, 640], replicated, may hold values from -0.5 to 0.5
- gain_mid: float32 [128], replicated, may hold values from 0.25 to 1.75
- w_mid: float32 [128, 128], replicated, may hold values from -0.5 to 0.5
- gain_second: float32 [128], replicated, may hold values from 0.25 to 1.75
- w_second: float32 [128, 512], replicated, may hold values from -0.5 to 0.5
- w_att_out: float32 [128, 128], replicated, may hold values from -0.5 to 0.5
Outputs:
- pair_out: float32 [256, 256, 128], P('row', 'col')
- pair_grad: float32 [256, 256, 128], P('row', 'col')
All inputs are finite; a program needn't handle non-finite values.
Results may differ from a plain program's by a relative error of at most 0.0003.
Values sent between devices are 32-bit elements; how exact they have to be, the bound alone decides.
A program may use at most 128 MiB of HBM per device.

v0:
```python
import math

import jax
import jax.numpy as jnp
from jax import lax
from jax.sharding import PartitionSpec as P

EPSILON = 1e-05
MASK_SHIFT = 1000000000.0
HIGHEST_PRECISION = lax.Precision.HIGHEST


def broadcast(block, axis, holder):
    block = jnp.where(lax.axis_index(axis) == holder, block, jnp.zeros_like(block))
    return lax.psum(block, axis)


def layer_norm(values, gain_vector):
    centre = values - jnp.mean(values, axis=-1, keepdims=True)
    spread = jnp.mean(centre * centre, axis=-1, keepdims=True)
    return centre * lax.rsqrt(spread + EPSILON) * gain_vector


def project(values, weight):
    return jnp.einsum("ijc,cd->ijd", values, weight, precision=HIGHEST_PRECISION)


def body(
    pair,
    cotangent,
    tri_bias,
    valid_length,
    gain_first,
    w_first,
    gain_mid,
    w_mid,
    gain_second,
    w_second,
    w_att_out,
):
    tile_rows = pair.shape[0]
    tile_cols = pair.shape[1]
    col_total = lax.axis_size("col")
    row_total = lax.axis_size("row")
    token_count = tile_cols * col_total
    row_index = lax.axis_index("row")
    col_index = lax.axis_index("col")
    mult_width = w_mid.shape[0]
    att_width = w_att_out.shape[0]
    head_count = tri_bias.shape[0]
    head_width = att_width // head_count
    valid_count = valid_length[0]
    all_valid = (jnp.arange(token_count) < valid_count).astype(jnp.float32)
    row_valid = (row_index * tile_rows + jnp.arange(tile_rows) < valid_count).astype(jnp.float32)
    col_valid = (col_index * tile_cols + jnp.arange(tile_cols) < valid_count).astype(jnp.float32)
    tile_mask = (row_valid[:, None] * col_valid[None, :])[:, :, None]
    score_scale = 1.0 / math.sqrt(head_width)
    key_shift = (all_valid - 1.0) * MASK_SHIFT

    def first_proj(values):
        projected = project(layer_norm(values, gain_first), w_first)
        left_part = (
            tile_mask
            * jax.nn.sigmoid(projected[..., :mult_width])
            * projected[..., mult_width : 2 * mult_width]
        )
        right_part = (
            tile_mask
            * jax.nn.sigmoid(projected[..., 2 * mult_width : 3 * mult_width])
            * projected[..., 3 * mult_width : 4 * mult_width]
        )
        return (left_part, right_part, jax.nn.sigmoid(projected[..., 4 * mult_width :]))

    def finish_mult(product, gate_part):
        return gate_part * project(layer_norm(product, gain_mid), w_mid)

    def second_proj(values):
        projected = project(layer_norm(values, gain_second), w_second)
        return (
            projected[..., :att_width],
            projected[..., att_width : 2 * att_width],
            projected[..., 2 * att_width : 3 * att_width],
            jax.nn.sigmoid(projected[..., 3 * att_width :]),
        )

    (left_factor, right_factor, out_gate), first_back = jax.vjp(first_proj, pair)
    left_panel, right_panel = (
        lax.all_gather(left_factor, "col", axis=1, tiled=True),
        lax.all_gather(right_factor, "col", axis=1, tiled=True),
    )
    col_ratio = col_total // row_total
    own_rows = lax.dynamic_slice_in_dim(
        right_panel, col_index % col_ratio * tile_cols, tile_cols, 0
    )
    right_cols = broadcast(own_rows, "row", col_index // col_ratio)
    product = jnp.einsum("ikc,jkc->ijc", left_panel, right_cols, precision=HIGHEST_PRECISION)
    update, mid_back = jax.vjp(finish_mult, product, out_gate)
    middle = pair + update
    (query, key_tile, value_tile, att_gate), second_back = jax.vjp(second_proj, middle)
    key_panel, value_panel = (
        lax.all_gather(key_tile, "col", axis=1, tiled=True),
        lax.all_gather(value_tile, "col", axis=1, tiled=True),
    )
    query_heads = query.reshape(tile_rows, tile_cols, head_count, head_width)
    key_heads = key_panel.reshape(tile_rows, token_count, head_count, head_width)
    value_heads = value_panel.reshape(tile_rows, token_count, head_count, head_width)
    scores = (
        jnp.einsum("ijhd,ikhd->ihjk", query_heads, key_heads, precision=HIGHEST_PRECISION)
        * score_scale
    )
    scores = scores + tri_bias[None] + key_shift[None, None, None, :]
    row_top = jnp.max(scores, axis=-1, keepdims=True)
    weights = jnp.exp(scores - row_top)
    weights = weights / jnp.sum(weights, axis=-1, keepdims=True)
    attended = jnp.einsum(
        "ihjk,ikhd->ijhd", weights, value_heads, precision=HIGHEST_PRECISION
    ).reshape(tile_rows, tile_cols, att_width)
    pair_out = middle + project(att_gate * attended, w_att_out)
    d_gated = jnp.einsum("ijc,dc->ijd", cotangent, w_att_out, precision=HIGHEST_PRECISION)
    d_att_gate = d_gated * attended
    d_attended = (d_gated * att_gate).reshape(tile_rows, tile_cols, head_count, head_width)
    d_weights = jnp.einsum("ijhd,ikhd->ihjk", d_attended, value_heads, precision=HIGHEST_PRECISION)
    d_scores = weights * (d_weights - jnp.sum(weights * d_weights, axis=-1, keepdims=True))
    d_query = (
        jnp.einsum("ihjk,ikhd->ijhd", d_scores, key_heads, precision=HIGHEST_PRECISION)
        * score_scale
    ).reshape(tile_rows, tile_cols, att_width)
    key_terms = (
        jnp.einsum("ihjk,ijhd->ikhd", d_scores, query_heads, precision=HIGHEST_PRECISION)
        * score_scale
    ).reshape(tile_rows, token_count, att_width)
    value_terms = jnp.einsum(
        "ihjk,ijhd->ikhd", weights, d_attended, precision=HIGHEST_PRECISION
    ).reshape(tile_rows, token_count, att_width)
    d_key, d_value = (
        lax.psum_scatter(key_terms, "col", scatter_dimension=1, tiled=True),
        lax.psum_scatter(value_terms, "col", scatter_dimension=1, tiled=True),
    )
    (d_second,) = second_back((d_query, d_key, d_value, d_att_gate))
    d_middle = cotangent + d_second
    d_product, d_out_gate = mid_back(d_middle)
    d_left = jnp.transpose(
        lax.psum_scatter(
            jnp.einsum("ijc,jkc->kic", d_product, right_cols, precision=HIGHEST_PRECISION),
            "col",
            scatter_dimension=0,
            tiled=True,
        ),
        (1, 0, 2),
    )
    right_terms = jnp.einsum("ijc,ikc->jkc", d_product, left_panel, precision=HIGHEST_PRECISION)
    right_total = lax.psum(right_terms, "row")
    right_moved = lax.all_to_all(right_total, "col", split_axis=1, concat_axis=0, tiled=True)
    d_right = lax.dynamic_slice_in_dim(right_moved, row_index * tile_rows, tile_rows, 0)
    (d_first,) = first_back((d_left, d_right, d_out_gate))
    pair_grad = d_middle + d_first
    return (pair_out, pair_grad)


def solution(mesh):
    return jax.shard_map(
        body,
        mesh=mesh,
        in_specs=(
            P("row", "col", None),
            P("row", "col", None),
            P(None, "col", None),
            P(),
            P(),
            P(),
            P(),
            P(),
            P(),
            P(),
            P(),
        ),
        out_specs=(P("row", "col", None), P("row", "col", None)),
        check_vma=False,
    )
```

profile of v0, /device:TPU:1, one launch (start us, length us, event | category | flops | bytes accessed | tf_op | source)
XLA Modules:
  0.0 777.0 jit_solution(8381677280629373884)
XLA Ops:
  15.7 59.8 %all-gather.5.cloned.1.call-done = f32[32,256,128]{2,1,0:T(8,128)} async-done(((f32[32,16,128]{2,1,0:T(8,128)}), f32[32,256,128]{2,1,0:T(8,128)}) %all-gather.5.cloned.1.call-update) | async-done | bytes 4194320 | tf_op jit(solution)/shard_map/all_gather | solution.py:89
  78.8 54.2 %all-gather.7.cloned.1.call-done = f32[32,256,128]{2,1,0:T(8,128)} async-done(((f32[32,16,128]{2,1,0:T(8,128)}), f32[32,256,128]{2,1,0:T(8,128)}) %all-gather.7.cloned.1.call-update) | async-done | bytes 4194320 | tf_op jit(solution)/shard_map/all_gather | solution.py:88
  133.0 14.5 %copy.121 = f32[32,256,128]{0,1,2:T(8,128)} copy(f32[32,256,128]{2,1,0:T(8,128)} %all-gather.7.cloned.1.call-done) | data formatting | bytes 8388608 | tf_op jit(solution)/shard_map/all_gather | solution.py:88
  147.5 63.7 %all-reduce.12.cloned.1.call-done = f32[16,256,128]{2,1,0:T(8,128)} async-done(((f32[16,256,128]{2,1,0:T(8,128)}), f32[16,256,128]{2,1,0:T(8,128)}) %all-reduce.12.cloned.1.call-update) | async-done | bytes 2097168 | tf_op jit(solution)/shard_map/psum | solution.py:15
  213.4 11.4 %fusion.97 = (f32[32,16]{0,1:T(8,128)S(1)}, f32[32,16,128]{0,1,2:T(8,128)S(1)}) fusion(f32[16,256,128]{1,0,2:T(8,128)S(1)} %copy.120, f32[32,256,128]{0,1,2:T(8,128)} %copy.121), kind=kOutput, calls=%fused_computation.143 | convolution fusion | flops 201391616 | bytes 6555648 | tf_op jit(solution)/shard_map/ikc,jkc->ijc/dot_general | solution.py:96
  243.3 57.5 %all-gather.11.cloned.1.call-done = f32[32,256,128]{2,1,0:T(8,128)} async-done(((f32[32,16,128]{2,1,0:T(8,128)}), f32[32,256,128]{2,1,0:T(8,128)}) %all-gather.11.cloned.1.call-update) | async-done | bytes 4194320 | tf_op jit(solution)/shard_map/all_gather | solution.py:101
  300.9 5.6 copy.128
  314.5 43.2 %all-gather.9.cloned.1.call-done = f32[32,256,128]{2,1,0:T(8,128)} async-done(((f32[32,16,128]{2,1,0:T(8,128)}), f32[32,256,128]{2,1,0:T(8,128)}) %all-gather.9.cloned.1.call-update) | async-done | bytes 4194320 | tf_op jit(solution)/shard_map/all_gather | solution.py:102
  357.6 5.6 copy.127
  363.2 6.9 convolution_bitcast_fusion.1
  378.7 6.3 multiply_reduce_fusion
  385.0 6.4 convolution_multiply_fusion
  391.4 5.6 copy.135
  397.5 8.3 %fusion.25 = f32[32,4,32,256]{3,2,1,0:T(8,128)} fusion(f32[32,16,4,32]{3,2,1,0:T(4,128)} %reshape.157, f32[32,4,16,256]{3,2,1,0:T(8,128)} %copy-done.8, f32[32,4,16]{2,1,0:T(4,128)} %fusion.1, f32[32,4,16]{2,1,0:T(4,128)} %copy-done.15), kind=kOutput, calls=%fused_computation.39 | convolution fusion | flops 202375168 | bytes 6569984 | tf_op jit(solution)/shard_map/ihjk,ijhd->ikhd/dot_general | solution.py:132
  405.8 5.8 copy.132
  411.7 8.0 %fusion.2 = f32[32,16,4,32]{3,1,2,0:T(8,128)S(1)} fusion(f32[32,256,4,32]{1,3,2,0:T(8,128)} %bitcast.71, f32[32,4,16,256]{3,2,1,0:T(8,128)} %copy-done.31, f32[32,4,16]{2,1,0:T(4,128)} %copy-done.32, f32[32,4,16,256]{3,2,1,0:T(8,128)} %copy-done.8, f32[32,4,16]{2,1,0:T(4,128)} %fusion.1, f32[32,4,16]{2,1,0:T(4,128)} %copy-done.15), kind=kOutput, calls=%fused_computation.11 | convolution fusion | flops 203489280 | bytes 8675328 | tf_op jit(solution)/shard_map/ihjk,ikhd->ijhd/dot_general | solution.py:125
  423.5 50.2 %reduce-scatter.6.cloned.1.call-done = f32[32,16,128]{2,1,0:T(8,128)} async-done(((f32[32,256,128]{2,1,0:T(8,128)}), f32[32,16,128]{2,1,0:T(8,128)}) %reduce-scatter.6.cloned.1.call-update) | async-done | bytes 262160 | tf_op jit(solution)/shard_map/reduce_scatter | solution.py:136
  473.8 84.0 %reduce-scatter.4.cloned.1.call-done = f32[32,16,128]{2,1,0:T(8,128)} async-done(((f32[32,256,128]{2,1,0:T(8,128)}), f32[32,16,128]{2,1,0:T(8,128)}) %reduce-scatter.4.cloned.1.call-update) | async-done | bytes 262160 | tf_op jit(solution)/shard_map/reduce_scatter | solution.py:137
  582.0 18.1 %convolution_bitcast_fusion = f32[16,256,128]{1,0,2:T(8,128)} fusion(f32[32,256,128]{0,1,2:T(8,128)} %copy.121, f32[32,16,128]{0,1,2:T(8,128)S(1)} %get-tuple-element.5, f32[32,16]{0,1:T(8,128)S(1)} %negate_multiply_fusion.1), kind=kOutput, calls=%fused_computation.8 | convolution fusion | flops 201392128 | bytes 6555648 | tf_op jit(solution)/shard_map/ijc,ikc->jkc/dot_general | solution.py:151
  606.5 5.3 copy.147
  611.8 66.9 %all-reduce.14.cloned.1.call-done = f32[16,256,128]{1,0,2:T(8,128)} async-done(((f32[16,256,128]{1,0,2:T(8,128)}), f32[16,256,128]{1,0,2:T(8,128)}) %all-reduce.14.cloned.1.call-update) | async-done | bytes 2097168 | tf_op jit(solution)/shard_map/psum | solution.py:152
  682.0 11.0 %all-to-all-start = ((f32[16,256,128]{2,0,1:T(8,128)}), f32[16,256,128]{2,0,1:T(8,128)S(1)}, u32[]{:S(2)}, u32[]{:S(2)}) async-start(f32[16,256,128]{2,0,1:T(8,128)} %copy.143), calls=%async_computation.2 | async-start | bytes 4194304 | tf_op jit(solution)/shard_map/all_to_all | solution.py:153
  695.1 26.4 %all-to-all-done = f32[16,256,128]{2,0,1:T(8,128)S(1)} async-done(((f32[16,256,128]{2,0,1:T(8,128)}), f32[16,256,128]{2,0,1:T(8,128)S(1)}, u32[]{:S(2)}, u32[]{:S(2)}) %all-to-all-start) | async-done | bytes 2097184 | tf_op jit(solution)/shard_map/all_to_all | solution.py:153
  726.6 39.4 %reduce-scatter.8.cloned.1.call-done = f32[16,32,128]{2,0,1:T(8,128)} async-done(((f32[256,32,128]{2,0,1:T(8,128)}), f32[16,32,128]{2,0,1:T(8,128)}) %reduce-scatter.8.cloned.1.call-update) | async-done | bytes 262160 | tf_op jit(solution)/shard_map/reduce_scatter | solution.py:143
  (153 shorter events, 97.8 us)
Async XLA Ops:
  7.2 68.4 %all-gather.5.cloned.1.call-start = ((), (), s32[]{:S(2)}) async-start(), calls=%async_computation.4 | async-start | bytes 4456448 | tf_op jit(solution)/shard_map/all_gather | solution.py:89
  10.4 68.3 %copy-start.23 = (f32[32,16]{0,1:T(8,128)}, f32[32,16]{0,1:T(8,128)S(1)}, u32[]{:S(2)}) copy-start(f32[32,16]{0,1:T(8,128)S(1)} %copy.118) | copy-start | bytes 6148
  10.6 68.1 %copy-start.19 = (f32[32,16]{1,0:T(8,128)}, f32[32,16]{1,0:T(8,128)S(1)}, u32[]{:S(2)}) copy-start(f32[32,16]{1,0:T(8,128)S(1)} %broadcast_multiply_fusion) | copy-start | bytes 6148
  14.9 118.1 %all-gather.7.cloned.1.call-start = ((), (), s32[]{:S(2)}) async-start(), calls=%async_computation.6 | async-start | bytes 4456448 | tf_op jit(solution)/shard_map/all_gather | solution.py:88
  15.6 195.5 %all-reduce.12.cloned.1.call-start = ((), (), s32[]{:S(2)}) async-start(), calls=%async_computation.5 | async-start | bytes 4194304 | tf_op jit(solution)/shard_map/psum | solution.py:15
  78.7 222.2 %all-gather.11.cloned.1.call-start = ((), (), s32[]{:S(2)}) async-start(), calls=%async_computation.8 | async-start | bytes 4456448 | tf_op jit(solution)/shard_map/all_gather | solution.py:101
  213.4 11.6 %copy-start.27 = (f32[128]{0:T(128)S(1)}, f32[128]{0:T(128)}, u32[]{:S(2)}) copy-start(f32[128]{0:T(128)} %param.17) | copy-start | bytes 1540
  239.6 118.0 %all-gather.9.cloned.1.call-start = ((), (), s32[]{:S(2)}) async-start(), calls=%async_computation.7 | async-start | bytes 4456448 | tf_op jit(solution)/shard_map/all_gather | solution.py:102
  240.2 233.6 %reduce-scatter.6.cloned.1.call-start = ((), (), s32[]{:S(2)}) async-start(), calls=%async_computation.10 | async-start | bytes 4456448 | tf_op jit(solution)/shard_map/reduce_scatter | solution.py:136
  378.7 6.3 copy-start.26
  385.0 6.4 copy-start.31
  385.0 6.4 copy-start.32
  397.1 160.7 %reduce-scatter.4.cloned.1.call-start = ((), (), s32[]{:S(2)}) async-start(), calls=%async_computation.9 | async-start | bytes 4456448 | tf_op jit(solution)/shard_map/reduce_scatter | solution.py:137
  411.6 267.1 %all-reduce.14.cloned.1.call-start = ((), (), s32[]{:S(2)}) async-start(), calls=%async_computation.11 | async-start | bytes 4194304 | tf_op jit(solution)/shard_map/psum | solution.py:152
  600.1 165.8 %reduce-scatter.8.cloned.1.call-start = ((), (), s32[]{:S(2)}) async-start(), calls=%async_computation.12 | async-start | bytes 4456448 | tf_op jit(solution)/shard_map/reduce_scatter | solution.py:143
  682.0 11.0 %copy-start.10 = (f32[32,16,128]{2,1,0:T(8,128)S(1)}, f32[32,16,128]{2,1,0:T(8,128)}, u32[]{:S(2)}) copy-start(f32[32,16,128]{2,1,0:T(8,128)} %get-tuple-element.7) | copy-start | bytes 786436
  682.0 11.0 %copy-start.17 = (f32[32,16,128]{2,1,0:T(8,128)S(1)}, f32[32,16,128]{2,1,0:T(8,128)}, u32[]{:S(2)}) copy-start(f32[32,16,128]{2,1,0:T(8,128)} %reshape.156) | copy-start | bytes 786436
  682.0 11.0 %copy-start.30 = (f32[128,128]{1,0:T(8,128)S(1)}, f32[128,128]{1,0:T(8,128)}, u32[]{:S(2)}) copy-start(f32[128,128]{1,0:T(8,128)} %param.21) | copy-start | bytes 196612
  682.0 39.4 %all-to-all-start = ((f32[16,256,128]{2,0,1:T(8,128)}), f32[16,256,128]{2,0,1:T(8,128)S(1)}, u32[]{:S(2)}, u32[]{:S(2)}) async-start(f32[16,256,128]{2,0,1:T(8,128)} %copy.143), calls=%async_computation.2 | async-start | bytes 4194304 | tf_op jit(solution)/shard_map/all_to_all | solution.py:153
  722.8 43.1 %copy-start.2 = (f32[32,16,640]{2,1,0:T(8,128)S(1)}, f32[32,16,640]{2,1,0:T(8,128)}, u32[]{:S(2)}) copy-start(f32[32,16,640]{2,1,0:T(8,128)} %copy-done.1) | copy-start | bytes 3932164
  722.8 43.1 %copy-start.20 = (f32[32,16]{1,0:T(8,128)S(1)}, f32[32,16]{1,0:T(8,128)}, u32[]{:S(2)}) copy-start(f32[32,16]{1,0:T(8,128)} %copy-done.19) | copy-start | bytes 6148
  726.5 40.7 %copy-start.6 = (f32[32,16,128]{2,1,0:T(8,128)S(1)}, f32[32,16,128]{2,1,0:T(8,128)}, u32[]{:S(2)}) copy-start(f32[32,16,128]{2,1,0:T(8,128)} %param.11) | copy-start | bytes 786436
  726.6 40.7 %copy-start.18 = (f32[32,16,128]{2,1,0:T(8,128)S(1)}, f32[32,16,128]{2,1,0:T(8,128)}, u32[]{:S(2)}) copy-start(f32[32,16,128]{2,1,0:T(8,128)} %get-tuple-element.2) | copy-start | bytes 786436
  726.6 40.7 %copy-start.29 = (f32[128]{0:T(128)S(1)}, f32[128]{0:T(128)}, u32[]{:S(2)}) copy-start(f32[128]{0:T(128)} %param.15) | copy-start | bytes 1540
  (19 other events, 54.1 us)
Sparse Core Ops, SparseCore 0:
  15.0 60.4 all-gather.4
  78.5 54.5 all-gather.6
  135.5 75.5 all-reduce.11
  239.7 61.1 all-gather.10
  303.1 54.5 all-gather.8
  397.2 76.5 reduce-scatter.5
  478.3 79.4 reduce-scatter.3
  600.2 78.4 all-reduce.13
  682.7 83.1 reduce-scatter.7
where the time goes:
time: 786 us; the launch traced here: 777 us
  waiting for transfers between devices  547 us (70%)
  matrix products  93.6 us (12%)
  local copies, waits for them, and re-layouts  85.7 us (11%)
  other arithmetic  23.8 us (3%)
  between operations  15.1 us (2%)
  starting transfers between devices  12.1 us (2%)
    reduce_scatter x1, waiting for transfers between devices, body(): lax.psum_scatter(value_terms, 'col', scatter_dimension=1, tiled=True)  84 us
    psum x1, waiting for transfers between devices, body(): right_total = lax.psum(right_terms, 'row')  66.9 us
    psum x1, waiting for transfers between devices, broadcast(): return lax.psum(block, axis)  63.7 us
    all_gather x1, waiting for transfers between devices, body(): lax.all_gather(right_factor, 'col', axis=1, tiled=True)  59.8 us
    all_gather x1, waiting for transfers between devices, body(): lax.all_gather(key_tile, 'col', axis=1, tiled=True)  57.5 us
    all_gather x1, waiting for transfers between devices, body(): lax.all_gather(left_factor, 'col', axis=1, tiled=True)  54.2 us
    reduce_scatter x1, waiting for transfers between devices, body(): lax.psum_scatter(key_terms, 'col', scatter_dimension=1, tiled=True)  50.2 us
    all_gather x1, waiting for transfers between devices, body(): lax.all_gather(value_tile, 'col', axis=1, tiled=True)  43.2 us
  transfers between devices with their start and end apart: 10, of which 10 were waited for; matrix products, arithmetic and copies ran while one was open for 10% of the time, Pallas kernels for 0%

commit v1 on v0

v1 whole, which is shorter than its diff:
```python
import functools
import math

import jax
import jax.numpy as jnp
from jax import lax
from jax.experimental import pallas as pl
from jax.experimental.pallas import tpu as pltpu
from jax.sharding import PartitionSpec as P

EPSILON = 1e-05
MASK_SHIFT = 1000000000.0
MESH = pl.DeviceIdType.MESH
F32 = jnp.float32
BF16 = jnp.bfloat16
NN = (((1,), (0,)), ((), ()))
NT = (((1,), (1,)), ((), ()))

T = 256
C = 128
HEADS = 4
WIDTH = 32
ROWS = 8
COLS = 16
N = ROWS * COLS
TI = T // ROWS
TJ = T // COLS
POS = TI * TJ
OWN = T // N


def split(x):
    hi = x.astype(BF16)
    return hi, (x - hi.astype(F32)).astype(BF16)


def dot(a, b, dims=NN):
    return lax.dot_general(a, b, dims, preferred_element_type=F32)


def mm(a, b, dims=NN):
    return dot(a[0], b[0], dims) + (dot(a[0], b[1], dims) + dot(a[1], b[0], dims))


def norm(u):
    centre = u - jnp.mean(u, axis=-1, keepdims=True)
    scale = lax.rsqrt(jnp.mean(centre * centre, axis=-1, keepdims=True) + EPSILON)
    return centre * scale, scale


def norm_back(d, xhat, scale):
    mean_d = jnp.mean(d, axis=-1, keepdims=True)
    mean_dx = jnp.mean(d * xhat, axis=-1, keepdims=True)
    return scale * (d - mean_d - xhat * mean_dx)


def swap_blocks(xs):
    block = lax.broadcasted_iota(jnp.int32, xs[0].shape, 1) // 32
    for bit in (2, 1):
        upper = (block & bit) != 0
        ys = list(xs)
        for s in range(4):
            if s & bit == 0:
                a, b = xs[s], xs[s | bit]
                ys[s] = jnp.where(upper, pltpu.roll(b, 32 * bit, 1), a)
                ys[s | bit] = jnp.where(upper, b, pltpu.roll(a, 128 - 32 * bit, 1))
        xs = ys
    return xs


def head_rows(x, h):
    zero = jnp.zeros((WIDTH, x.shape[1]), x.dtype)
    return jnp.concatenate([x[WIDTH * h : WIDTH * (h + 1)] if g == h else zero for g in range(HEADS)], axis=0)


def kernel(
    valid_ref,
    pair_ref,
    cot_ref,
    bias_ref,
    gain_first,
    w_first,
    gain_mid,
    w_mid,
    gain_second,
    w_second,
    w_att_out,
    out_ref,
    grad_ref,
    send_a,
    recv_a,
    send_x,
    recv_x,
    send_d,
    recv_d,
    send_g,
    recv_g,
    pair_r,
    cot_r,
    bias_r,
    bias_t,
    out_r,
    grad_r,
    grad_t,
    xhat_t,
    scale_t,
    proj_t,
    mask_t,
    at_s,
    bt_s,
    at_hi,
    at_lo,
    bt_hi,
    bt_lo,
    dx_s,
    e_hi,
    e_lo,
    ph_r,
    ps_r,
    g1_r,
    dgated_r,
    sem_in,
    a_sems,
    x_sems,
    d_sems,
    g_sems,
    pair_sems,
    cot_sems,
    bias_sems,
    out_sems,
    grad_sems,
):
    r = lax.axis_index("row")
    c = lax.axis_index("col")
    me = r * COLS + c
    valid = valid_ref[0]

    barrier = pltpu.get_barrier_semaphore()

    def greet_col(i, _):
        pl.semaphore_signal(barrier, inc=1, device_id=(r, lax.rem(c + i, COLS)), device_id_type=MESH)
        return 0

    def greet_row(i, _):
        pl.semaphore_signal(barrier, inc=1, device_id=(lax.rem(r + i, ROWS), c), device_id_type=MESH)
        return 0

    lax.fori_loop(1, COLS, greet_col, 0)
    lax.fori_loop(1, ROWS, greet_row, 0)

    def send_all(src, dst, sems):
        def go(i, _):
            d = lax.rem(me + i, N)
            pltpu.make_async_remote_copy(
                src(d), dst, sems.at[0], sems.at[1], device_id=(d // COLS, lax.rem(d, COLS)), device_id_type=MESH
            ).start()
            return 0

        lax.fori_loop(1, N, go, 0)

    def send_cols(src, dst, sems):
        def go(i, _):
            d = lax.rem(c + i, COLS)
            pltpu.make_async_remote_copy(
                src(d), dst, sems.at[0], sems.at[1], device_id=(r, d), device_id_type=MESH
            ).start()
            return 0

        lax.fori_loop(1, COLS, go, 0)

    def waiter(view, sems):
        return pltpu.make_async_remote_copy(view, view, sems.at[0], sems.at[1], device_id=(r, c), device_id_type=MESH)

    pair_flat = pair_ref.reshape(POS, C)
    u = jnp.concatenate([pair_flat[pl.ds(kk, TI, stride=TJ)] for kk in range(TJ)], axis=0)
    xhat, scale = norm(u)
    xhat_t[...] = xhat
    scale_t[...] = jnp.broadcast_to(scale, (POS, C))
    w03 = split(w_first[:, : 4 * C])
    proj = mm(split(xhat * gain_first[...]), w03)
    pos = lax.broadcasted_iota(jnp.int32, (POS, C), 0)
    in_row = (r * TI + pos % TI) < valid
    in_col = (c * TJ + pos // TI) < valid
    mask = jnp.where(in_row & in_col, 1.0, 0.0).astype(F32)
    mask_t[...] = mask
    sig0 = jax.nn.sigmoid(proj[:, :C])
    sig2 = jax.nn.sigmoid(proj[:, 2 * C : 3 * C])
    p1 = proj[:, C : 2 * C]
    p3 = proj[:, 3 * C :]
    proj_t[0] = sig0
    proj_t[1] = p1
    proj_t[2] = sig2
    proj_t[3] = p3
    left = mask * sig0 * p1
    right = mask * sig2 * p3
    sa = send_a.reshape(N * 8, C)
    for q in range(4):
        sa[pl.ds(q, C, stride=8)] = left[128 * q : 128 * (q + 1)].T
        sa[pl.ds(4 + q, C, stride=8)] = right[128 * q : 128 * (q + 1)].T

    pl.semaphore_wait(barrier, COLS - 1 + ROWS - 1)

    def greet_again(i, _):
        pl.semaphore_signal(sem_in, inc=1, device_id=(lax.rem(r + i, ROWS), c), device_id_type=MESH)
        return 0

    lax.fori_loop(1, ROWS, greet_again, 0)
    pl.semaphore_wait(sem_in, ROWS - 1)

    send_all(lambda d: send_a.at[d], recv_a.at[me], a_sems)
    recv_a[me] = send_a[me]

    pair_view = pair_ref.reshape(OWN, TJ, TJ, C)
    cot_view = cot_ref.reshape(OWN, TJ, TJ, C)
    here = pl.ds(pl.multiple_of(c * TJ, TJ), TJ)
    send_cols(lambda d: pair_view.at[:, d], pair_r.at[:, here], pair_sems)
    send_cols(lambda d: cot_view.at[:, d], cot_r.at[:, here], cot_sems)
    send_cols(lambda d: bias_ref, bias_r.at[:, here], bias_sems)
    pair_r[:, here] = pair_view[:, c]
    cot_r[:, here] = cot_view[:, c]
    bias_r[:, here] = bias_ref[...]

    waiter(recv_a.at[pl.ds(0, N - 1)], a_sems).wait_recv()
    ra = recv_a.reshape(N * 8, C)
    for part, dest in ((0, at_s), (4, bt_s)):
        for half in range(2):
            for q in range(4):
                ys = swap_blocks(
                    [ra[pl.ds((64 * half + 16 * rr) * 8 + part + q, COLS, stride=8)] for rr in range(4)]
                )
                for g in range(4):
                    dest[pl.ds((4 * q + g) * COLS, COLS), pl.ds(128 * half, 128)] = ys[g]
    at = at_s[...]
    a_parts = split(at.T)
    at_parts = split(at)
    at_hi[...], at_lo[...] = at_parts
    bt_parts = split(bt_s[...])
    bt_hi[...], bt_lo[...] = bt_parts
    x = mm(a_parts, bt_parts)
    for l in range(OWN):
        sx = send_x.at[l].reshape(N * 8, C)
        for rr in range(ROWS):
            for jh in range(2):
                sx[pl.ds(16 * rr * 8 + jh, COLS, stride=8)] = x[
                    TI * rr + 16 * l : TI * rr + 16 * (l + 1), 128 * jh : 128 * (jh + 1)
                ]
        send_all(lambda d: send_x.at[l, d, pl.ds(0, 2)], recv_x.at[l, me, pl.ds(0, 2)], x_sems.at[l])
        recv_x[l, me] = send_x[l, me]

    waiter(pair_r.reshape(OWN * T, C).at[pl.ds(0, OWN * TJ * (COLS - 1))], pair_sems).wait_recv()
    waiter(cot_r.reshape(OWN * T, C).at[pl.ds(0, OWN * TJ * (COLS - 1))], cot_sems).wait_recv()
    w4 = split(w_first[:, 4 * C :])
    w_out = split(w_att_out[...])
    for l in range(OWN):
        ph, ps = norm(pair_r[l])
        ph_r[l] = ph
        ps_r[l] = jnp.broadcast_to(ps, (T, C))
        g1_r[l] = jax.nn.sigmoid(mm(split(ph * gain_first[...]), w4))
        dgated_r[l] = mm(split(cot_r[l]), w_out, NT)
    waiter(bias_r.reshape(HEADS * T, T).at[pl.ds(0, HEADS * TJ * (COLS - 1))], bias_sems).wait_recv()
    key = lax.broadcasted_iota(jnp.int32, (T, T), 0)
    shift = jnp.where(key < valid, 0.0, -MASK_SHIFT).astype(F32)
    for h in range(HEADS):
        bias_t[h] = bias_r[h].T + shift

    w_sec = split(w_second[...])
    w_m = split(w_mid[...])
    score_scale = 1.0 / math.sqrt(WIDTH)

    def row(l, _):
        waiter(recv_x.at[l, pl.ds(0, N - 1), pl.ds(0, 2)], x_sems.at[l]).wait_recv()
        rx = recv_x.at[l].reshape(N * 8, C)
        x = jnp.concatenate([rx[pl.ds(jh, C, stride=8)].T for jh in range(2)], axis=0)
        xh, xs = norm(x)
        m = mm(split(xh * gain_mid[...]), w_m)
        g1 = g1_r[l]
        z1 = pair_r[l] + g1 * m
        zh, zs = norm(z1)
        second = mm(split(zh * gain_second[...]), w_sec)
        q = second[:, :C] * score_scale
        k = second[:, C : 2 * C]
        v = second[:, 2 * C : 3 * C]
        g2 = jax.nn.sigmoid(second[:, 3 * C :])
        k_hi, k_lo = split(k)
        v_hi, v_lo = split(v)
        q_hi, q_lo = split(q)
        qt_hi, qt_lo = split(q.T)
        kt_hi, kt_lo = split(k.T)
        vt_hi, vt_lo = split(v.T)
        k_both = jnp.concatenate([k_hi, k_lo], axis=1)
        v_both = jnp.concatenate([v_hi, v_lo], axis=1)
        ots = []
        inverses = []
        for h in range(HEADS):
            hs = slice(WIDTH * h, WIDTH * (h + 1))
            top = head_rows(qt_hi, h)
            s = dot(k_both, jnp.concatenate([top, top], axis=0)) + dot(k_hi, head_rows(qt_lo, h))
            s = s + bias_t[h]
            e = jnp.exp(s - jnp.max(s, axis=0, keepdims=True))
            inverse = 1.0 / jnp.sum(e, axis=0, keepdims=True)
            eh, el = split(e)
            e_hi[h] = eh
            e_lo[h] = el
            both = dot(jnp.concatenate([vt_hi[hs], vt_lo[hs]], axis=0), eh)
            ot = both[:WIDTH] + (both[WIDTH:] + dot(vt_hi[hs], el))
            ots.append(ot * inverse)
            inverses.append(inverse)
        ot = jnp.concatenate(ots, axis=0)
        o = ot.T
        out_r[l] = z1 + mm(split(g2 * o), w_out)
        send_cols(
            lambda d: out_r.at[l, pl.ds(pl.multiple_of(d * TJ, TJ), TJ)], out_ref.at[l * TJ + c], out_sems.at[l]
        )
        out_ref[l * TJ + c] = out_r[l, here]

        dgated = dgated_r[l]
        d_o = dgated * g2
        d_s = dgated * o * g2 * (1.0 - g2)
        d_ot = d_o.T
        d_ots = []
        deltas = []
        for h in range(HEADS):
            hs = slice(WIDTH * h, WIDTH * (h + 1))
            part = d_ot[hs] * inverses[h]
            deltas.append(jnp.sum(part * ots[h], axis=0, keepdims=True))
            d_ots.append(part)
        d_ots = jnp.concatenate(d_ots, axis=0)
        d_os_hi, d_os_lo = split(d_ots.T)
        dt_hi, dt_lo = split(d_ots)
        lane = lax.broadcasted_iota(jnp.int32, (T, C), 1) // WIDTH
        zero = jnp.zeros((T, C), BF16)
        dk = jnp.zeros((T, 2 * C), F32)
        dv = jnp.zeros((T, 2 * C), F32)
        dk_low = jnp.zeros((T, C), F32)
        dv_low = jnp.zeros((T, C), F32)
        dqs = []
        for h in range(HEADS):
            hs = slice(WIDTH * h, WIDTH * (h + 1))
            own = lane == h
            top = head_rows(dt_hi, h)
            dp = dot(v_both, jnp.concatenate([top, top], axis=0)) + dot(v_hi, head_rows(dt_lo, h))
            eh = e_hi[h]
            el = e_lo[h]
            ds = (eh.astype(F32) + el.astype(F32)) * (dp - deltas[h])
            dsh, dsl = split(ds)
            both = dot(jnp.concatenate([kt_hi[hs], kt_lo[hs]], axis=0), dsh)
            dqs.append(both[:WIDTH] + (both[WIDTH:] + dot(kt_hi[hs], dsl)))
            qm_hi = jnp.where(own, q_hi, zero)
            qm_lo = jnp.where(own, q_lo, zero)
            dk = dk + dot(dsh, jnp.concatenate([qm_hi, qm_lo], axis=1))
            dk_low = dk_low + dot(dsl, qm_hi)
            om_hi = jnp.where(own, d_os_hi, zero)
            om_lo = jnp.where(own, d_os_lo, zero)
            dv = dv + dot(eh, jnp.concatenate([om_hi, om_lo], axis=1))
            dv_low = dv_low + dot(el, om_hi)
        dq = jnp.concatenate(dqs, axis=0).T * score_scale
        dk = dk[:, :C] + (dk[:, C:] + dk_low)
        dv = dv[:, :C] + (dv[:, C:] + dv_low)
        d_second = jnp.concatenate([dq, dk, dv, d_s], axis=1)
        du2 = mm(split(d_second), w_sec, NT) * gain_second[...]
        dz1 = cot_r[l] + norm_back(du2, zh, zs)
        du = mm(split(dz1 * g1), w_m, NT) * gain_mid[...]
        dx = norm_back(du, xh, xs)
        sd = send_d.at[l].reshape(N * 8, C)
        for jh in range(2):
            sd[pl.ds(jh, C, stride=8)] = dx[128 * jh : 128 * (jh + 1)].T
        send_all(lambda d: send_d.at[l, d, pl.ds(0, 2)], recv_d.at[l, me, pl.ds(0, 2)], d_sems.at[l])
        recv_d[l, me] = send_d[l, me]
        dp4 = dz1 * m * g1 * (1.0 - g1)
        grad_r[l] = dz1 + norm_back(mm(split(dp4), w4, NT) * gain_first[...], ph_r[l], ps_r[l])
        send_cols(
            lambda d: grad_r.at[l, pl.ds(pl.multiple_of(d * TJ, TJ), TJ)], grad_t.at[l * TJ + c], grad_sems.at[l]
        )
        grad_t[l * TJ + c] = grad_r[l, here]
        return 0

    lax.fori_loop(0, OWN, row, 0)

    for l in range(OWN):
        waiter(recv_d.at[l, pl.ds(0, N - 1), pl.ds(0, 2)], d_sems.at[l]).wait_recv()
        rd = recv_d.at[l].reshape(N * 8, C)
        for rr in range(ROWS):
            for jh in range(2):
                dx_s[pl.ds(TI * rr + 16 * l, 16), pl.ds(128 * jh, 128)] = rd[pl.ds(16 * rr * 8 + jh, COLS, stride=8)]
    dx_parts = split(dx_s[...])
    d_bt = mm((at_hi[...], at_lo[...]), dx_parts)
    d_at = mm((bt_hi[...], bt_lo[...]), dx_parts, NT)
    sg = send_g.reshape(N * 8, C)
    for part, d_src in ((0, d_at), (4, d_bt)):
        for half in range(2):
            for q in range(4):
                ys = swap_blocks(
                    [
                        d_src[(4 * q + g) * COLS : (4 * q + g + 1) * COLS, 128 * half : 128 * (half + 1)]
                        for g in range(4)
                    ]
                )
                for rr in range(4):
                    sg[pl.ds((64 * half + 16 * rr) * 8 + part + q, COLS, stride=8)] = ys[rr]
    send_all(lambda d: send_g.at[d], recv_g.at[me], g_sems)
    recv_g[me] = send_g[me]

    waiter(recv_g.at[pl.ds(0, N - 1)], g_sems).wait_recv()
    rg = recv_g.reshape(N * 8, C)
    mask = mask_t[...]
    da = jnp.concatenate([rg[pl.ds(q, C, stride=8)].T for q in range(4)], axis=0) * mask
    db = jnp.concatenate([rg[pl.ds(4 + q, C, stride=8)].T for q in range(4)], axis=0) * mask
    sig0 = proj_t[0]
    sig2 = proj_t[2]
    dp1 = da * sig0
    dp3 = db * sig2
    dp0 = dp1 * proj_t[1] * (1.0 - sig0)
    dp2 = dp3 * proj_t[3] * (1.0 - sig2)
    d_proj = jnp.concatenate([dp0, dp1, dp2, dp3], axis=1)
    w03 = split(w_first[:, : 4 * C])
    du = mm(split(d_proj), w03, NT) * gain_first[...]
    res = norm_back(du, xhat_t[...], scale_t[...])
    grad_flat = grad_ref.reshape(POS, C)
    part_flat = grad_t.reshape(POS, C)
    for l in range(OWN):
        waiter(grad_t.at[pl.ds(0, COLS - 1)], grad_sems.at[l]).wait_recv()
    for kk in range(TJ):
        grad_flat[pl.ds(kk, TI, stride=TJ)] = res[TI * kk : TI * (kk + 1)] + part_flat[pl.ds(kk, TI, stride=TJ)]

    waiter(recv_a.at[pl.ds(0, N - 1)], a_sems).wait_send()
    waiter(pair_r.reshape(OWN * T, C).at[pl.ds(0, OWN * TJ * (COLS - 1))], pair_sems).wait_send()
    waiter(cot_r.reshape(OWN * T, C).at[pl.ds(0, OWN * TJ * (COLS - 1))], cot_sems).wait_send()
    waiter(bias_r.reshape(HEADS * T, T).at[pl.ds(0, HEADS * TJ * (COLS - 1))], bias_sems).wait_send()
    waiter(recv_g.at[pl.ds(0, N - 1)], g_sems).wait_send()
    for l in range(OWN):
        waiter(recv_x.at[l, pl.ds(0, N - 1), pl.ds(0, 2)], x_sems.at[l]).wait_send()
        waiter(recv_d.at[l, pl.ds(0, N - 1), pl.ds(0, 2)], d_sems.at[l]).wait_send()
        waiter(grad_t.at[pl.ds(0, COLS - 1)], grad_sems.at[l]).wait_send()
        waiter(out_ref.at[pl.ds(0, COLS - 1)], out_sems.at[l]).wait()


def body(pair, cotangent, tri_bias, valid_length, gain_first, w_first, gain_mid, w_mid, gain_second, w_second, w_att_out):
    vmem = pl.BlockSpec(memory_space=pltpu.VMEM)
    smem = pl.BlockSpec(memory_space=pltpu.SMEM)
    tile = jax.ShapeDtypeStruct((TI, TJ, C), F32)
    message = pltpu.VMEM((N, 8, C), F32)
    halves = pltpu.VMEM((OWN, N, 8, C), F32)
    rows = pltpu.VMEM((OWN, T, C), F32)
    square = pltpu.VMEM((T, T), F32)
    square_low = pltpu.VMEM((T, T), BF16)
    pair_of = pltpu.SemaphoreType.DMA((2,))
    pairs_of = pltpu.SemaphoreType.DMA((OWN, 2))
    return pl.pallas_call(
        kernel,
        out_shape=(tile, tile),
        in_specs=[smem] + [vmem] * 10,
        out_specs=(vmem, vmem),
        scratch_shapes=[
            message,
            message,
            halves,
            halves,
            halves,
            halves,
            message,
            message,
            rows,
            rows,
            pltpu.VMEM((HEADS, T, T), F32),
            pltpu.VMEM((HEADS, T, T), F32),
            rows,
            rows,
            pltpu.VMEM((TI, TJ, C), F32),
            pltpu.VMEM((POS, C), F32),
            pltpu.VMEM((POS, C), F32),
            pltpu.VMEM((4, POS, C), F32),
            pltpu.VMEM((POS, C), F32),
            square,
            square,
            square_low,
            square_low,
            square_low,
            square_low,
            square,
            pltpu.VMEM((HEADS, T, T), BF16),
            pltpu.VMEM((HEADS, T, T), BF16),
            rows,
            rows,
            rows,
            rows,
            pltpu.SemaphoreType.REGULAR,
            pair_of,
            pairs_of,
            pairs_of,
            pair_of,
            pair_of,
            pair_of,
            pair_of,
            pairs_of,
            pairs_of,
        ],
        compiler_params=pltpu.CompilerParams(
            collective_id=0, has_side_effects=True, vmem_limit_bytes=48 * 1024 * 1024
        ),
        cost_estimate=pl.CostEstimate(flops=2_000_000_000, bytes_accessed=4_000_000, transcendentals=1_000_000),
    )(
        valid_length,
        pair,
        cotangent,
        tri_bias,
        gain_first.reshape(1, C),
        w_first,
        gain_mid.reshape(1, C),
        w_mid,
        gain_second.reshape(1, C),
        w_second,
        w_att_out,
    )


def solution(mesh):
    return jax.shard_map(
        body,
        mesh=mesh,
        in_specs=(
            P("row", "col", None),
            P("row", "col", None),
            P(None, "col", None),
            P(),
            P(),
            P(),
            P(),
            P(),
            P(),
            P(),
            P(),
        ),
        out_specs=(P("row", "col", None), P("row", "col", None)),
        check_vma=False,
    )
```

time: 786 us -> 84.6 us (0.11); the launches traced: 777 us -> 84.2 us
  waiting for transfers between devices: 547 us -> 0 us
  matrix products: 93.6 us -> 0 us
  local copies, waits for them, and re-layouts: 85.7 us -> 8.41 us
  Pallas kernels: 0 us -> 74.4 us
  other arithmetic: 23.8 us -> 0 us
  between operations: 15.1 us -> 1.32 us
  starting transfers between devices: 12.1 us -> 0 us
    all_gather x4 -> x0, waiting for transfers between devices: 215 us -> none  [the longest x1 59.8 us: body(): lax.all_gather(right_factor, 'col', axis=1, tiled=True)]
    reduce_scatter x3 -> x0, waiting for transfers between devices: 174 us -> none  [the longest x1 84 us: body(): lax.psum_scatter(value_terms, 'col', scatter_dimension=1, tiled=True)]
    psum x2 -> x0, waiting for transfers between devices: 131 us -> none  [the longest x1 66.9 us: body(): right_total = lax.psum(right_terms, 'row')]
    dot_general x17 -> x0, matrix products: 93.6 us -> none  [the longest x1 18.1 us: body(): jnp.einsum('ijc,ikc->jkc', d_product, left_panel, precision=HIGHEST_PRECI...]
    pallas_call x0 -> x1, Pallas kernels: none -> 74.4 us  [body(): pl.pallas_call(kernel, out_shape=(tile, tile), in_specs=[smem] + [vmem] *...]
    all_to_all x1 -> x0, waiting for transfers between devices: 26.4 us -> none  [body(): lax.all_to_all(right_total, 'col', split_axis=1, concat_axis=0, tiled=True)]
    all_gather x3 -> x0, local copies, waits for them, and re-layouts: 25.7 us -> none  [the longest x1 14.5 us: body(): lax.all_gather(left_factor, 'col', axis=1, tiled=True)]
    reshape x6 -> x0, local copies, waits for them, and re-layouts: 21 us -> none  [the longest x1 5.8 us: body(): value_terms = jnp.einsum('ihjk,ijhd->ikhd', weights, d_attended, precisio...]
  transfers between devices with their start and end apart: 10 -> 0, of which waited for: 10 -> 0; matrix products, arithmetic and copies ran while one was open for 10% -> 0% of each run, Pallas kernels for 0% -> 0%
where the time goes in v1:
time: 84.6 us; the launch traced here: 84.2 us
  Pallas kernels  74.4 us (88%)
  local copies, waits for them, and re-layouts  8.41 us (10%)
  between operations  1.32 us (2%)
    pallas_call x1, Pallas kernels, body(): pl.pallas_call(kernel, out_shape=(tile, tile), in_specs=[smem] + [vmem] *...  74.4 us
    unnamed x22, local copies, waits for them, and re-layouts  8.41 us

profile of v1, /device:TPU:1, one launch (start us, length us, event | category | flops | bytes accessed | tf_op | source)
XLA Modules:
  0.0 84.2 jit_solution(2819848174456260699)
XLA Ops:
  1.3 0.0 copy-start.7
  1.3 0.0 copy-start.8
  1.3 0.0 copy-start.9
  1.3 0.6 copy-done.7
  1.9 0.0 copy-done.8
  2.0 0.0 copy-done.9
  2.0 0.0 copy-start
  2.0 1.0 %copy-done = f32[128,640]{1,0:T(8,128)S(1)} copy-done((f32[128,640]{1,0:T(8,128)S(1)}, f32[128,640]{1,0:T(8,128)}, u32[]{:S(2)}) %copy-start) | copy-done | bytes 327704
  2.9 0.0 copy-start.1
  2.9 0.9 %copy-done.1 = f32[32,16,128]{2,1,0:T(8,128)S(1)} copy-done((f32[32,16,128]{2,1,0:T(8,128)S(1)}, f32[32,16,128]{2,1,0:T(8,128)}, u32[]{:S(2)}) %copy-start.1) | copy-done | bytes 262168
  3.9 0.0 copy-start.2
  3.9 0.9 %copy-done.2 = f32[32,16,128]{2,1,0:T(8,128)S(1)} copy-done((f32[32,16,128]{2,1,0:T(8,128)S(1)}, f32[32,16,128]{2,1,0:T(8,128)}, u32[]{:S(2)}) %copy-start.2) | copy-done | bytes 262168
  4.8 0.0 copy-start.3
  4.8 0.9 %copy-done.3 = f32[128,512]{1,0:T(8,128)S(1)} copy-done((f32[128,512]{1,0:T(8,128)S(1)}, f32[128,512]{1,0:T(8,128)}, u32[]{:S(2)}) %copy-start.3) | copy-done | bytes 262168
  5.8 0.0 copy-start.4
  5.8 0.8 copy-done.4
  6.6 0.0 copy-start.5
  6.6 0.8 copy-done.5
  7.5 0.0 copy-start.6
  7.5 0.8 copy-done.6
  8.3 74.4 %shard_map.122 = (f32[32,16,128]{2,1,0:T(8,128)S(1)}, f32[32,16,128]{2,1,0:T(8,128)S(1)}) custom-call(s32[1]{0:T(128)S(6)} %copy.15.valid_ref, f32[32,16,128]{2,1,0:T(8,128)S(1)} %copy-done.1, f32[32,16,128]{2,1,0:T(8,128)S(1)} %copy-done.2, f32[4,16,256]{2,1,0:T(8,128)S(1)} %copy-done.4, f32[1,128]{1,0:T(1,128)S(1)} %bitcast.3, f32[128,640]{1,0:T(8,128)S(1)} %copy-done, ...), custom_call_target="tpu_custom_call" | custom-call | flops 2000000000 | bytes 4000000 | tf_op jit(solution)/shard_map/pallas_call | solution.py:448
  82.8 0.7 copy.16
  83.5 0.7 copy.17
Async XLA Ops:
  1.3 0.7 copy-start.7
  1.3 0.7 copy-start.8
  1.3 0.7 copy-start.9
  2.0 1.0 %copy-start = (f32[128,640]{1,0:T(8,128)S(1)}, f32[128,640]{1,0:T(8,128)}, u32[]{:S(2)}) copy-start(f32[128,640]{1,0:T(8,128)} %w_first.1) | copy-start | bytes 983044
  2.9 0.9 %copy-start.1 = (f32[32,16,128]{2,1,0:T(8,128)S(1)}, f32[32,16,128]{2,1,0:T(8,128)}, u32[]{:S(2)}) copy-start(f32[32,16,128]{2,1,0:T(8,128)} %pair_ref.1) | copy-start | bytes 786436
  3.9 0.9 %copy-start.2 = (f32[32,16,128]{2,1,0:T(8,128)S(1)}, f32[32,16,128]{2,1,0:T(8,128)}, u32[]{:S(2)}) copy-start(f32[32,16,128]{2,1,0:T(8,128)} %cot_ref.1) | copy-start | bytes 786436
  4.8 0.9 %copy-start.3 = (f32[128,512]{1,0:T(8,128)S(1)}, f32[128,512]{1,0:T(8,128)}, u32[]{:S(2)}) copy-start(f32[128,512]{1,0:T(8,128)} %w_second.1) | copy-start | bytes 786436
  5.8 0.8 copy-start.4
  6.6 0.8 copy-start.5
  7.5 0.8 copy-start.6

commit v2 on v1

v2 whole, which is shorter than its diff:
```python
import functools
import math

import jax
import jax.numpy as jnp
from jax import lax
from jax.experimental import pallas as pl
from jax.experimental.pallas import tpu as pltpu
from jax.sharding import PartitionSpec as P

EPSILON = 1e-05
MASK_SHIFT = 1000000000.0
MESH = pl.DeviceIdType.MESH
F32 = jnp.float32
BF16 = jnp.bfloat16
NN = (((1,), (0,)), ((), ()))
NT = (((1,), (1,)), ((), ()))

T = 256
C = 128
HEADS = 4
WIDTH = 32
ROWS = 8
COLS = 16
N = ROWS * COLS
TI = T // ROWS
TJ = T // COLS
POS = TI * TJ
OWN = T // N


def split(x):
    hi = x.astype(BF16)
    return hi, (x - hi.astype(F32)).astype(BF16)


def dot(a, b, dims=NN):
    return lax.dot_general(a, b, dims, preferred_element_type=F32)


def mm(a, b, dims=NN):
    return dot(a[0], b[0], dims) + (dot(a[0], b[1], dims) + dot(a[1], b[0], dims))


def norm(u):
    centre = u - jnp.mean(u, axis=0, keepdims=True)
    scale = lax.rsqrt(jnp.mean(centre * centre, axis=0, keepdims=True) + EPSILON)
    return centre * scale, scale


def norm_back(d, xhat, scale):
    mean_d = jnp.mean(d, axis=0, keepdims=True)
    mean_dx = jnp.mean(d * xhat, axis=0, keepdims=True)
    return scale * (d - mean_d - xhat * mean_dx)


def left3(x):
    hi, lo = split(x)
    return jnp.concatenate([hi, lo, hi], axis=1)


def right3(x):
    hi, lo = split(x)
    return jnp.concatenate([hi, hi, lo], axis=0)


def turn(x):
    rows, cols = x.shape
    return jnp.concatenate(
        [
            jnp.concatenate([x[128 * i : 128 * (i + 1), 128 * j : 128 * (j + 1)].T for i in range(rows // 128)], axis=1)
            for j in range(cols // 128)
        ],
        axis=0,
    )


def swap_blocks(xs):
    block = lax.broadcasted_iota(jnp.int32, xs[0].shape, 1) // 32
    for bit in (2, 1):
        upper = (block & bit) != 0
        ys = list(xs)
        for s in range(4):
            if s & bit == 0:
                a, b = xs[s], xs[s | bit]
                ys[s] = jnp.where(upper, pltpu.roll(b, 32 * bit, 1), a)
                ys[s | bit] = jnp.where(upper, b, pltpu.roll(a, 128 - 32 * bit, 1))
        xs = ys
    return xs


def head_keys(x):
    hi = x.astype(BF16).astype(F32)
    again = pltpu.roll(hi, WIDTH, 1)
    lo = pltpu.roll(x - hi, 2 * WIDTH, 1)
    block = lax.broadcasted_iota(jnp.int32, x.shape, 1) // WIDTH
    return [
        jnp.where(block == h, hi, jnp.where(block == (h + 1) % HEADS, again, lo)).astype(BF16) for h in range(HEADS)
    ]


def head_queries(hi, lo, h):
    own = slice(WIDTH * h, WIDTH * (h + 1))
    blocks = [None] * HEADS
    blocks[h] = hi[own]
    blocks[(h + 1) % HEADS] = lo[own]
    blocks[(h + 2) % HEADS] = hi[own]
    blocks[(h + 3) % HEADS] = jnp.zeros_like(hi[own])
    return jnp.concatenate(blocks, axis=0)


def kernel(
    valid_ref,
    pair_any,
    cot_any,
    bias_any,
    gain_first,
    w_first_any,
    gain_mid,
    w_mid_any,
    gain_second,
    w_second_any,
    w_att_out_any,
    out_ref,
    grad_ref,
    send_a,
    recv_a,
    send_x,
    recv_x,
    send_d,
    recv_d,
    send_g,
    recv_g,
    pair_r,
    cot_r,
    bias_r,
    bias_t,
    out_r,
    grad_r,
    grad_t,
    xhat_t,
    scale_t,
    proj_t,
    mask_t,
    at_s,
    bt_s,
    at_hi,
    at_lo,
    bt_hi,
    bt_lo,
    dx_s,
    e_s,
    e_hi,
    e_lo,
    w03_s,
    w4_s,
    w4t_s,
    wm_s,
    wmt_s,
    wo_s,
    wot_s,
    w2_s,
    w2t_s,
    pair_ref,
    w_first,
    w_mid,
    w_second,
    w_att_out,
    sem_in,
    load_sems,
    a_sems,
    x_sems,
    d_sems,
    g_sems,
    pair_sems,
    cot_sems,
    bias_sems,
    twin_sems,
    out_sems,
    grad_sems,
):
    r = lax.axis_index("row")
    c = lax.axis_index("col")
    me = r * COLS + c
    valid = valid_ref[0]

    barrier = pltpu.get_barrier_semaphore()

    def greet_col(i, _):
        pl.semaphore_signal(barrier, inc=1, device_id=(r, lax.rem(c + i, COLS)), device_id_type=MESH)
        return 0

    def greet_row(i, _):
        pl.semaphore_signal(barrier, inc=1, device_id=(lax.rem(r + i, ROWS), c), device_id_type=MESH)
        return 0

    lax.fori_loop(1, COLS, greet_col, 0)
    lax.fori_loop(1, ROWS, greet_row, 0)

    here = pl.ds(pl.multiple_of(c * TJ, TJ), TJ)
    cot_view = cot_any.reshape(OWN, TJ, TJ, C)
    loads = [
        pltpu.make_async_copy(src, dst, load_sems.at[n])
        for n, (src, dst) in enumerate(
            (
                (pair_any, pair_ref),
                (w_first_any, w_first),
                (bias_any, bias_r.at[:, here]),
                (w_second_any, w_second),
                (w_mid_any, w_mid),
                (w_att_out_any, w_att_out),
                (cot_view.at[:, c], cot_r.at[:, here]),
            )
        )
    ]
    for load in loads:
        load.start()

    def send_all(src, dst, sems):
        def go(i, _):
            d = lax.rem(me + i, N)
            pltpu.make_async_remote_copy(
                src(d), dst, sems.at[0], sems.at[1], device_id=(d // COLS, lax.rem(d, COLS)), device_id_type=MESH
            ).start()
            return 0

        lax.fori_loop(1, N, go, 0)

    def send_cols(src, dst, sems):
        def go(i, _):
            d = lax.rem(c + i, COLS)
            pltpu.make_async_remote_copy(
                src(d), dst, sems.at[0], sems.at[1], device_id=(r, d), device_id_type=MESH
            ).start()
            return 0

        lax.fori_loop(1, COLS, go, 0)

    def waiter(view, sems):
        return pltpu.make_async_remote_copy(view, view, sems.at[0], sems.at[1], device_id=(r, c), device_id_type=MESH)

    for load in loads[:2]:
        load.wait()
    pair_flat = pair_ref.reshape(POS, C)
    u = jnp.concatenate(
        [
            jnp.concatenate([pair_flat[pl.ds(4 * q + g, TI, stride=TJ)] for g in range(4)], axis=0).T
            for q in range(4)
        ],
        axis=1,
    )
    xhat, scale = norm(u)
    xhat_t[...] = xhat
    scale_t[...] = jnp.broadcast_to(scale, (8, POS))
    gain = jnp.broadcast_to(gain_first[...], (C, C)).T
    w03 = w_first[:, : 4 * C] * jnp.concatenate([gain] * 4, axis=1)
    w03_s[...] = left3(w03)
    proj = dot(left3(turn(w03)), right3(xhat))
    pos = lax.broadcasted_iota(jnp.int32, (8, POS), 1)
    in_row = (r * TI + pos % TI) < valid
    in_col = (c * TJ + pos // TI) < valid
    mask_t[...] = jnp.where(in_row & in_col, 1.0, 0.0).astype(F32)
    mask = mask_t[0:1]
    sig0 = jax.nn.sigmoid(proj[:C])
    sig2 = jax.nn.sigmoid(proj[2 * C : 3 * C])
    p1 = proj[C : 2 * C]
    p3 = proj[3 * C :]
    proj_t[0] = sig0
    proj_t[1] = p1
    proj_t[2] = sig2
    proj_t[3] = p3
    left = mask * sig0 * p1
    right = mask * sig2 * p3
    sa = send_a.reshape(N * 8, C)
    for q in range(4):
        sa[pl.ds(q, C, stride=8)] = left[:, 128 * q : 128 * (q + 1)]
        sa[pl.ds(4 + q, C, stride=8)] = right[:, 128 * q : 128 * (q + 1)]

    for load in loads[3:6]:
        load.wait()
    w4 = w_first[:, 4 * C :] * gain
    w4_s[...] = left3(w4)
    w4t_s[...] = left3(w4.T)
    w_m = w_mid[...] * jnp.broadcast_to(gain_mid[...], (C, C)).T
    wm_s[...] = left3(w_m)
    wmt_s[...] = left3(w_m.T)
    wo_s[...] = left3(w_att_out[...])
    wot_s[...] = left3(w_att_out[...].T)
    w_sec = w_second[...] * jnp.concatenate([jnp.broadcast_to(gain_second[...], (C, C)).T] * 4, axis=1)
    w2_s[...] = left3(w_sec)
    w2t_s[...] = left3(turn(w_sec))

    pl.semaphore_wait(barrier, COLS - 1 + ROWS - 1)

    def greet_again(i, _):
        pl.semaphore_signal(sem_in, inc=1, device_id=(lax.rem(r + i, ROWS), c), device_id_type=MESH)
        return 0

    lax.fori_loop(1, ROWS, greet_again, 0)
    pl.semaphore_wait(sem_in, ROWS - 1)
    send_all(lambda d: send_a.at[d], recv_a.at[me], a_sems)
    recv_a[me] = send_a[me]

    pair_view = pair_ref.reshape(OWN, TJ, TJ, C)

    def send_bias(i, _):
        d = lax.rem(c + 2 * i, COLS)
        pltpu.make_async_remote_copy(
            bias_any, bias_r.at[:, here], bias_sems.at[0], bias_sems.at[1], device_id=(r, d), device_id_type=MESH
        ).start()
        return 0

    send_cols(lambda d: pair_view.at[:, d], pair_r.at[:, here], pair_sems)
    lax.fori_loop(1, COLS // 2, send_bias, 0)
    pair_r[:, here] = pair_view[:, c]

    waiter(recv_a.at[pl.ds(0, N - 1)], a_sems).wait_recv()
    ra = recv_a.reshape(N * 8, C)
    for part, dest in ((0, at_s), (4, bt_s)):
        for half in range(2):
            for q in range(4):
                ys = swap_blocks(
                    [ra[pl.ds((64 * half + 16 * rr) * 8 + part + q, COLS, stride=8)] for rr in range(4)]
                )
                for g in range(4):
                    dest[pl.ds((4 * q + g) * COLS, COLS), pl.ds(128 * half, 128)] = ys[g]
    at = at_s[...]
    a_parts = split(at.T)
    at_parts = split(at)
    at_hi[...], at_lo[...] = at_parts
    bt_parts = split(bt_s[...])
    bt_hi[...], bt_lo[...] = bt_parts
    x = mm(a_parts, bt_parts)
    sx = send_x.reshape(N * 8, C)
    for l in range(OWN):
        for rr in range(ROWS):
            for jh in range(2):
                sx[pl.ds(16 * rr * 8 + 2 * l + jh, COLS, stride=8)] = x[
                    TI * rr + 16 * l : TI * rr + 16 * (l + 1), 128 * jh : 128 * (jh + 1)
                ]
    send_all(lambda d: send_x.at[d, pl.ds(0, 4)], recv_x.at[me, pl.ds(0, 4)], x_sems)
    recv_x[me] = send_x[me]

    send_cols(lambda d: cot_view.at[:, d], cot_r.at[:, here], cot_sems)
    half_bias = COLS // 2 - 1
    waiter(bias_r.reshape(HEADS * T, T).at[pl.ds(0, HEADS * TJ * half_bias)], bias_sems).wait_recv()
    loads[2].wait()
    odd = lax.rem(c, 2)
    bias_view = bias_r.reshape(HEADS, COLS // 2, 2, TJ, T)
    pltpu.make_async_remote_copy(
        bias_view.at[:, :, odd],
        bias_view.at[:, :, odd],
        twin_sems.at[0],
        twin_sems.at[1],
        device_id=(r, c + 1 - 2 * odd),
        device_id_type=MESH,
    ).start()
    waiter(pair_r.reshape(OWN * T, C).at[pl.ds(0, OWN * TJ * (COLS - 1))], pair_sems).wait_recv()
    pair_t = turn(pair_r.reshape(OWN * T, C)[...])
    ph, ps = norm(pair_t)
    g1 = jax.nn.sigmoid(dot(w4t_s[...], right3(ph)))
    waiter(bias_r.reshape(HEADS * T, T).at[pl.ds(0, HEADS * T // 2)], twin_sems).wait_recv()
    key = lax.broadcasted_iota(jnp.int32, (T, T), 0)
    shift = jnp.where(key < valid, 0.0, -MASK_SHIFT).astype(F32)
    for h in range(HEADS):
        bias_t[h] = bias_r[h].T + shift

    waiter(recv_x.at[pl.ds(0, N - 1), pl.ds(0, 4)], x_sems).wait_recv()
    rx = recv_x.reshape(N * 8, C)
    x = jnp.concatenate([rx[pl.ds(m, C, stride=8)] for m in range(4)], axis=1)
    xh, xs = norm(x)
    m = dot(wmt_s[...], right3(xh))
    z1 = pair_t + g1 * m
    zh, zs = norm(z1)
    second = dot(w2t_s[...], right3(zh))
    score_scale = 1.0 / math.sqrt(WIDTH)
    qt_hi, qt_lo = split(second[:C] * score_scale)
    kt_hi, kt_lo = split(second[C : 2 * C])
    vt_hi, vt_lo = split(second[2 * C : 3 * C])
    g2 = jax.nn.sigmoid(second[3 * C :])
    ots = [[], []]
    inverses = [[], []]
    for l in range(OWN):
        js = slice(T * l, T * (l + 1))
        keys = head_keys(turn(second[C : 2 * C, js]))
        for h in range(HEADS):
            hs = slice(WIDTH * h, WIDTH * (h + 1))
            s = dot(keys[h], head_queries(qt_hi[:, js], qt_lo[:, js], h)) + bias_t[h]
            e = jnp.exp(s - jnp.max(s, axis=0, keepdims=True))
            inverse = 1.0 / jnp.sum(e, axis=0, keepdims=True)
            eh, el = split(e)
            e_s[l, h] = e
            e_hi[l, h] = eh
            e_lo[l, h] = el
            both = dot(jnp.concatenate([vt_hi[hs, js], vt_lo[hs, js]], axis=0), eh)
            ots[l].append((both[:WIDTH] + (both[WIDTH:] + dot(vt_hi[hs, js], el))) * inverse)
            inverses[l].append(inverse)
    o = jnp.concatenate([jnp.concatenate(ots[l], axis=0) for l in range(OWN)], axis=1)

    for load in loads[6:]:
        load.wait()
    waiter(cot_r.reshape(OWN * T, C).at[pl.ds(0, OWN * TJ * (COLS - 1))], cot_sems).wait_recv()
    cot = turn(cot_r.reshape(OWN * T, C)[...])
    dgated = dot(wo_s[...], right3(cot))
    d_o = dgated * g2
    d_s = dgated * o * g2 * (1.0 - g2)
    dqs = [[], []]
    dks = [[], []]
    dvs = [[], []]
    for l in range(OWN):
        js = slice(T * l, T * (l + 1))
        values = head_keys(turn(second[2 * C : 3 * C, js]))
        for h in range(HEADS):
            hs = slice(WIDTH * h, WIDTH * (h + 1))
            part = d_o[hs, js] * inverses[l][h]
            delta = jnp.sum(part * ots[l][h], axis=0, keepdims=True)
            dt_hi, dt_lo = split(part)
            zero = jnp.zeros_like(dt_hi)
            blocks = [None] * HEADS
            for n, block in enumerate((dt_hi, dt_lo, dt_hi, zero)):
                blocks[(h + n) % HEADS] = block
            dp = dot(values[h], jnp.concatenate(blocks, axis=0))
            dsh, dsl = split(e_s[l, h] * (dp - delta))
            both = dot(jnp.concatenate([kt_hi[hs, js], kt_lo[hs, js]], axis=0), dsh)
            dqs[l].append(both[:WIDTH] + (both[WIDTH:] + dot(kt_hi[hs, js], dsl)))
            both = dot(jnp.concatenate([qt_hi[hs, js], qt_lo[hs, js]], axis=0), dsh, NT)
            dks[l].append(both[:WIDTH] + (both[WIDTH:] + dot(qt_hi[hs, js], dsl, NT)))
            both = dot(jnp.concatenate([dt_hi, dt_lo], axis=0), e_hi[l, h], NT)
            dvs[l].append(both[:WIDTH] + (both[WIDTH:] + dot(dt_hi, e_lo[l, h], NT)))

    def stack(parts):
        return jnp.concatenate([jnp.concatenate(parts[l], axis=0) for l in range(OWN)], axis=1)

    d_second = jnp.concatenate([stack(dqs) * score_scale, stack(dks), stack(dvs), d_s], axis=0)
    dz1 = cot + norm_back(dot(w2_s[...], right3(d_second)), zh, zs)
    dx = norm_back(dot(wm_s[...], right3(dz1 * g1)), xh, xs)
    sd = send_d.reshape(N * 8, C)
    for n in range(4):
        sd[pl.ds(n, C, stride=8)] = dx[:, 128 * n : 128 * (n + 1)]
    send_all(lambda d: send_d.at[d, pl.ds(0, 4)], recv_d.at[me, pl.ds(0, 4)], d_sems)
    recv_d[me] = send_d[me]

    out_flat = out_r.reshape(OWN * T, C)
    grad_part = grad_r.reshape(OWN * T, C)
    out_flat[...] = turn(z1 + dot(wot_s[...], right3(g2 * o)))
    for l in range(OWN):
        send_cols(
            lambda d: out_r.at[l, pl.ds(pl.multiple_of(d * TJ, TJ), TJ)], out_ref.at[l * TJ + c], out_sems.at[l]
        )
        out_ref[l * TJ + c] = out_r[l, here]
    dp4 = dz1 * m * g1 * (1.0 - g1)
    grad_part[...] = turn(dz1 + norm_back(dot(w4_s[...], right3(dp4)), ph, ps))
    for l in range(OWN):
        send_cols(
            lambda d: grad_r.at[l, pl.ds(pl.multiple_of(d * TJ, TJ), TJ)], grad_t.at[l * TJ + c], grad_sems.at[l]
        )
        grad_t[l * TJ + c] = grad_r[l, here]

    waiter(recv_d.at[pl.ds(0, N - 1), pl.ds(0, 4)], d_sems).wait_recv()
    rd = recv_d.reshape(N * 8, C)
    for l in range(OWN):
        for rr in range(ROWS):
            for jh in range(2):
                dx_s[pl.ds(TI * rr + 16 * l, 16), pl.ds(128 * jh, 128)] = rd[
                    pl.ds(16 * rr * 8 + 2 * l + jh, COLS, stride=8)
                ]
    dx_parts = split(dx_s[...])
    d_bt = mm((at_hi[...], at_lo[...]), dx_parts)
    d_at = mm((bt_hi[...], bt_lo[...]), dx_parts, NT)
    sg = send_g.reshape(N * 8, C)
    for part, d_src in ((0, d_at), (4, d_bt)):
        for half in range(2):
            for q in range(4):
                ys = swap_blocks(
                    [
                        d_src[(4 * q + g) * COLS : (4 * q + g + 1) * COLS, 128 * half : 128 * (half + 1)]
                        for g in range(4)
                    ]
                )
                for rr in range(4):
                    sg[pl.ds((64 * half + 16 * rr) * 8 + part + q, COLS, stride=8)] = ys[rr]
    send_all(lambda d: send_g.at[d], recv_g.at[me], g_sems)
    recv_g[me] = send_g[me]

    waiter(recv_g.at[pl.ds(0, N - 1)], g_sems).wait_recv()
    rg = recv_g.reshape(N * 8, C)
    mask = mask_t[0:1]
    da = jnp.concatenate([rg[pl.ds(q, C, stride=8)] for q in range(4)], axis=1) * mask
    db = jnp.concatenate([rg[pl.ds(4 + q, C, stride=8)] for q in range(4)], axis=1) * mask
    sig0 = proj_t[0]
    sig2 = proj_t[2]
    dp1 = da * sig0
    dp3 = db * sig2
    dp0 = dp1 * proj_t[1] * (1.0 - sig0)
    dp2 = dp3 * proj_t[3] * (1.0 - sig2)
    du = dot(w03_s[...], right3(jnp.concatenate([dp0, dp1, dp2, dp3], axis=0)))
    res = turn(norm_back(du, xhat_t[...], scale_t[0:1]))
    grad_flat = grad_ref.reshape(POS, C)
    part_flat = grad_t.reshape(POS, C)
    for l in range(OWN):
        waiter(grad_t.at[pl.ds(0, COLS - 1)], grad_sems.at[l]).wait_recv()
    for kk in range(TJ):
        grad_flat[pl.ds(kk, TI, stride=TJ)] = res[TI * kk : TI * (kk + 1)] + part_flat[pl.ds(kk, TI, stride=TJ)]

    waiter(recv_a.at[pl.ds(0, N - 1)], a_sems).wait_send()
    waiter(pair_r.reshape(OWN * T, C).at[pl.ds(0, OWN * TJ * (COLS - 1))], pair_sems).wait_send()
    waiter(cot_r.reshape(OWN * T, C).at[pl.ds(0, OWN * TJ * (COLS - 1))], cot_sems).wait_send()
    waiter(bias_r.reshape(HEADS * T, T).at[pl.ds(0, HEADS * TJ * half_bias)], bias_sems).wait_send()
    waiter(bias_r.reshape(HEADS * T, T).at[pl.ds(0, HEADS * T // 2)], twin_sems).wait_send()
    waiter(recv_g.at[pl.ds(0, N - 1)], g_sems).wait_send()
    waiter(recv_x.at[pl.ds(0, N - 1), pl.ds(0, 4)], x_sems).wait_send()
    waiter(recv_d.at[pl.ds(0, N - 1), pl.ds(0, 4)], d_sems).wait_send()
    for l in range(OWN):
        waiter(grad_t.at[pl.ds(0, COLS - 1)], grad_sems.at[l]).wait_send()
        waiter(out_ref.at[pl.ds(0, COLS - 1)], out_sems.at[l]).wait()


def body(pair, cotangent, tri_bias, valid_length, gain_first, w_first, gain_mid, w_mid, gain_second, w_second, w_att_out):
    vmem = pl.BlockSpec(memory_space=pltpu.VMEM)
    smem = pl.BlockSpec(memory_space=pltpu.SMEM)
    anywhere = pl.BlockSpec(memory_space=pl.ANY)
    tile = jax.ShapeDtypeStruct((TI, TJ, C), F32)
    message = pltpu.VMEM((N, 8, C), F32)
    weight = pltpu.VMEM((C, 3 * C), BF16)
    rows = pltpu.VMEM((OWN, T, C), F32)
    square = pltpu.VMEM((T, T), F32)
    square_low = pltpu.VMEM((T, T), BF16)
    pair_of = pltpu.SemaphoreType.DMA((2,))
    pairs_of = pltpu.SemaphoreType.DMA((OWN, 2))
    return pl.pallas_call(
        kernel,
        out_shape=(tile, tile),
        in_specs=[smem] + [anywhere] * 3 + [vmem, anywhere] * 3 + [anywhere],
        out_specs=(vmem, vmem),
        scratch_shapes=[
            message,
            message,
            message,
            message,
            message,
            message,
            message,
            message,
            rows,
            rows,
            pltpu.VMEM((HEADS, T, T), F32),
            pltpu.VMEM((HEADS, T, T), F32),
            rows,
            rows,
            pltpu.VMEM((TI, TJ, C), F32),
            pltpu.VMEM((C, POS), F32),
            pltpu.VMEM((8, POS), F32),
            pltpu.VMEM((4, C, POS), F32),
            pltpu.VMEM((8, POS), F32),
            square,
            square,
            square_low,
            square_low,
            square_low,
            square_low,
            square,
            pltpu.VMEM((OWN, HEADS, T, T), F32),
            pltpu.VMEM((OWN, HEADS, T, T), BF16),
            pltpu.VMEM((OWN, HEADS, T, T), BF16),
            pltpu.VMEM((C, 12 * C), BF16),
            weight,
            weight,
            weight,
            weight,
            weight,
            weight,
            pltpu.VMEM((C, 12 * C), BF16),
            pltpu.VMEM((4 * C, 3 * C), BF16),
            pltpu.VMEM((TI, TJ, C), F32),
            pltpu.VMEM((C, 5 * C), F32),
            pltpu.VMEM((C, C), F32),
            pltpu.VMEM((C, 4 * C), F32),
            pltpu.VMEM((C, C), F32),
            pltpu.SemaphoreType.REGULAR,
            pltpu.SemaphoreType.DMA((7,)),
            pair_of,
            pair_of,
            pair_of,
            pair_of,
            pair_of,
            pair_of,
            pair_of,
            pair_of,
            pairs_of,
            pairs_of,
        ],
        compiler_params=pltpu.CompilerParams(
            collective_id=0, has_side_effects=True, vmem_limit_bytes=60 * 1024 * 1024
        ),
        cost_estimate=pl.CostEstimate(flops=2_000_000_000, bytes_accessed=4_000_000, transcendentals=1_000_000),
    )(
        valid_length,
        pair,
        cotangent,
        tri_bias,
        gain_first.reshape(1, C),
        w_first,
        gain_mid.reshape(1, C),
        w_mid,
        gain_second.reshape(1, C),
        w_second,
        w_att_out,
    )


def solution(mesh):
    return jax.shard_map(
        body,
        mesh=mesh,
        in_specs=(
            P("row", "col", None),
            P("row", "col", None),
            P(None, "col", None),
            P(),
            P(),
            P(),
            P(),
            P(),
            P(),
            P(),
            P(),
        ),
        out_specs=(P("row", "col", None), P("row", "col", None)),
        check_vma=False,
    )
```

time: 84.6 us -> 70.6 us (0.83)
  Pallas kernels: 74.4 us -> 66.7 us
  local copies, waits for them, and re-layouts: 8.41 us -> 2.42 us
    pallas_call x1, Pallas kernels: 74.4 us -> 66.7 us  [body(): pl.pallas_call(kernel, out_shape=(tile, tile), in_specs=[smem] + [anywher...]
    unnamed x22 -> x4, local copies, waits for them, and re-layouts: 8.41 us -> 2.42 us
where the time goes in v2:
time: 70.6 us; the launch traced here: 70.4 us
  Pallas kernels  66.7 us (94%)
  local copies, waits for them, and re-layouts  2.42 us (3%)
  between operations  1.3 us (2%)
    pallas_call x1, Pallas kernels, body(): pl.pallas_call(kernel, out_shape=(tile, tile), in_specs=[smem] + [anywher...  66.7 us
    unnamed x4, local copies, waits for them, and re-layouts  2.42 us

profile of v2, /device:TPU:1, one launch (start us, length us, event | category | flops | bytes accessed | tf_op | source)
XLA Modules:
  0.0 70.4 jit_solution(16949759192825240946)
XLA Ops:
  1.3 66.7 %shard_map.122 = (f32[32,16,128]{2,1,0:T(8,128)}, f32[32,16,128]{2,1,0:T(8,128)}) custom-call(s32[1]{0:T(128)S(6)} %copy.15.valid_ref, f32[32,16,128]{2,1,0:T(8,128)} %pair_any.1, f32[32,16,128]{2,1,0:T(8,128)} %cot_any.1, f32[4,16,256]{2,1,0:T(8,128)} %bias_any.1, f32[1,128]{1,0:T(1,128)} %bitcast.3, f32[128,640]{1,0:T(8,128)} %w_first_any.1, ...), custom_call_target="tpu_custom_call" | custom-call | flops 2000000000 | bytes 4000000 | tf_op jit(solution)/shard_map/pallas_call | solution.py:530
  68.0 0.0 copy-start
  68.0 1.7 %copy.16 = f32[32,16,128]{2,1,0:T(8,128)} copy(f32[32,16,128]{2,1,0:T(8,128)} %get-tuple-element.4) | data formatting | bytes 524288
  69.7 0.0 copy-done
  69.7 0.7 copy.17
Async XLA Ops:
  68.0 1.7 %copy-start = (f32[32,16,128]{2,1,0:T(8,128)S(1)}, f32[32,16,128]{2,1,0:T(8,128)}, u32[]{:S(2)}) copy-start(f32[32,16,128]{2,1,0:T(8,128)} %get-tuple-element.5) | copy-start | bytes 786436

commit v3 on v2

--- a/solution.py
+++ b/solution.py
@@ -310,8 +310,8 @@
         ).start()
         return 0
 
+    lax.fori_loop(1, COLS // 2, send_bias, 0)
     send_cols(lambda d: pair_view.at[:, d], pair_r.at[:, here], pair_sems)
-    lax.fori_loop(1, COLS // 2, send_bias, 0)
     pair_r[:, here] = pair_view[:, c]
 
     waiter(recv_a.at[pl.ds(0, N - 1)], a_sems).wait_recv()
@@ -397,6 +397,14 @@
             inverses[l].append(inverse)
     o = jnp.concatenate([jnp.concatenate(ots[l], axis=0) for l in range(OWN)], axis=1)
 
+    out_flat = out_r.reshape(OWN * T, C)
+    out_flat[...] = turn(z1 + dot(wot_s[...], right3(g2 * o)))
+    for l in range(OWN):
+        send_cols(
+            lambda d: out_r.at[l, pl.ds(pl.multiple_of(d * TJ, TJ), TJ)], out_ref.at[l * TJ + c], out_sems.at[l]
+        )
+        out_ref[l * TJ + c] = out_r[l, here]
+
     for load in loads[6:]:
         load.wait()
     waiter(cot_r.reshape(OWN * T, C).at[pl.ds(0, OWN * TJ * (COLS - 1))], cot_sems).wait_recv()
@@ -440,14 +448,7 @@
     send_all(lambda d: send_d.at[d, pl.ds(0, 4)], recv_d.at[me, pl.ds(0, 4)], d_sems)
     recv_d[me] = send_d[me]
 
-    out_flat = out_r.reshape(OWN * T, C)
     grad_part = grad_r.reshape(OWN * T, C)
-    out_flat[...] = turn(z1 + dot(wot_s[...], right3(g2 * o)))
-    for l in range(OWN):
-        send_cols(
-            lambda d: out_r.at[l, pl.ds(pl.multiple_of(d * TJ, TJ), TJ)], out_ref.at[l * TJ + c], out_sems.at[l]
-        )
-        out_ref[l * TJ + c] = out_r[l, here]
     dp4 = dz1 * m * g1 * (1.0 - g1)
     grad_part[...] = turn(dz1 + norm_back(dot(w4_s[...], right3(dp4)), ph, ps))
     for l in range(OWN):

time: 70.6 us -> 64.6 us (0.915)
  Pallas kernels: 66.7 us -> 60.7 us
    pallas_call x1, Pallas kernels: 66.7 us -> 60.7 us  [body(): pl.pallas_call(kernel, out_shape=(tile, tile), in_specs=[smem] + [anywher...]
where the time goes in v3:
time: 64.6 us; the launch traced here: 64.4 us
  Pallas kernels  60.7 us (94%)
  local copies, waits for them, and re-layouts  2.42 us (4%)
  between operations  1.3 us (2%)
    pallas_call x1, Pallas kernels, body(): pl.pallas_call(kernel, out_shape=(tile, tile), in_specs=[smem] + [anywher...  60.7 us
    unnamed x4, local copies, waits for them, and re-layouts  2.42 us

profile of v3, /device:TPU:1, one launch (start us, length us, event | category | flops | bytes accessed | tf_op | source)
XLA Modules:
  0.0 64.4 jit_solution(621843717909480117)
XLA Ops:
  1.3 60.7 %shard_map.122 = (f32[32,16,128]{2,1,0:T(8,128)}, f32[32,16,128]{2,1,0:T(8,128)}) custom-call(s32[1]{0:T(128)S(6)} %copy.15.valid_ref, f32[32,16,128]{2,1,0:T(8,128)} %pair_any.1, f32[32,16,128]{2,1,0:T(8,128)} %cot_any.1, f32[4,16,256]{2,1,0:T(8,128)} %bias_any.1, f32[1,128]{1,0:T(1,128)} %bitcast.3, f32[128,640]{1,0:T(8,128)} %w_first_any.1, ...), custom_call_target="tpu_custom_call" | custom-call | flops 2000000000 | bytes 4000000 | tf_op jit(solution)/shard_map/pallas_call | solution.py:531
  62.0 0.0 copy-start
  62.0 1.7 %copy.16 = f32[32,16,128]{2,1,0:T(8,128)} copy(f32[32,16,128]{2,1,0:T(8,128)} %get-tuple-element.4) | data formatting | bytes 524288
  63.7 0.0 copy-done
  63.7 0.7 %copy.17 = f32[32,16,128]{2,1,0:T(8,128)} copy(f32[32,16,128]{2,1,0:T(8,128)S(1)} %copy-done) | data formatting | bytes 524288
Async XLA Ops:
  62.0 1.7 %copy-start = (f32[32,16,128]{2,1,0:T(8,128)S(1)}, f32[32,16,128]{2,1,0:T(8,128)}, u32[]{:S(2)}) copy-start(f32[32,16,128]{2,1,0:T(8,128)} %get-tuple-element.5) | copy-start | bytes 786436

commit v4 on v3

--- a/solution.py
+++ b/solution.py
@@ -1,4 +1,4 @@
-import functools
+import itertools
 import math
 
 import jax
@@ -114,23 +114,27 @@
     pair_any,
     cot_any,
     bias_any,
-    gain_first,
+    gain_first_any,
     w_first_any,
-    gain_mid,
+    gain_mid_any,
     w_mid_any,
-    gain_second,
+    gain_second_any,
     w_second_any,
     w_att_out_any,
     out_ref,
     grad_ref,
     send_a,
     recv_a,
+    send_b,
+    recv_b,
     send_x,
     recv_x,
     send_d,
     recv_d,
-    send_g,
-    recv_g,
+    send_ga,
+    recv_ga,
+    send_gb,
+    recv_gb,
     pair_r,
     cot_r,
     bias_r,
@@ -166,12 +170,17 @@
     w_mid,
     w_second,
     w_att_out,
+    gain_first,
+    gain_mid,
+    gain_second,
     sem_in,
     load_sems,
     a_sems,
+    b_sems,
     x_sems,
     d_sems,
-    g_sems,
+    ga_sems,
+    gb_sems,
     pair_sems,
     cot_sems,
     bias_sems,
@@ -186,16 +195,22 @@
 
     barrier = pltpu.get_barrier_semaphore()
 
-    def greet_col(i, _):
-        pl.semaphore_signal(barrier, inc=1, device_id=(r, lax.rem(c + i, COLS)), device_id_type=MESH)
+    def column(t):
+        near = lax.div(t, 8)
+        step = lax.div(lax.rem(t, 8), 2)
+        z = lax.rem(lax.div(c, 4) + 2 + 3 * step + 3 * lax.div(step * (step - 1), 2), 4)
+        hi = lax.rem(lax.div(c, 2) + 1 - near, 2)
+        core = lax.rem(c + 1 - lax.rem(t, 2), 2)
+        return 4 * z + 2 * hi + core
+
+    def greet_col(t, _):
+        pl.semaphore_signal(barrier, inc=1, device_id=(r, column(t)), device_id_type=MESH)
         return 0
 
     def greet_row(i, _):
         pl.semaphore_signal(barrier, inc=1, device_id=(lax.rem(r + i, ROWS), c), device_id_type=MESH)
         return 0
 
-    lax.fori_loop(1, COLS, greet_col, 0)
-    lax.fori_loop(1, ROWS, greet_row, 0)
 
     here = pl.ds(pl.multiple_of(c * TJ, TJ), TJ)
     cot_view = cot_any.reshape(OWN, TJ, TJ, C)
@@ -205,6 +220,9 @@
             (
                 (pair_any, pair_ref),
                 (w_first_any, w_first),
+                (gain_first_any, gain_first),
+                (gain_mid_any, gain_mid),
+                (gain_second_any, gain_second),
                 (bias_any, bias_r.at[:, here]),
                 (w_second_any, w_second),
                 (w_mid_any, w_mid),
@@ -216,30 +234,59 @@
     for load in loads:
         load.start()
 
+    x_at = lax.rem(lax.div(c, 2), 2) * 2 + lax.div(r, 4)
+    xs_at = [lax.rem(x_at + n, 4) for n in range(4)]
+    row_of_x = [4 * lax.rem(v, 2) for v in xs_at]
+    col_of_x = [2 * lax.div(v, 2) for v in xs_at]
+    row_of_y = [lax.rem(lax.rem(r, 4) + n, 4) for n in range(4)]
+    col_of_z = [4 * lax.rem(lax.div(c, 4) + n, 4) for n in range(4)]
+
+    def for_all(visit):
+        for hops in sorted(itertools.product(range(3), repeat=3), key=lambda h: -sum(h)):
+            ones = [axis for axis in range(3) if hops[axis] == 1]
+
+            def go(t, _):
+                def pick(options, axis):
+                    if axis not in ones:
+                        return options[hops[axis]]
+                    sign = lax.rem(lax.div(t, 2 ** (1 + ones.index(axis))), 2)
+                    return options[1] + sign * (options[3] - options[1])
+
+                row = pick(row_of_x, 0) + pick(row_of_y, 1)
+                core = lax.rem(c + lax.rem(t, 2), 2)
+                col = pick(col_of_x, 0) + pick(col_of_z, 2) + core
+                visit(row, col)
+                return 0
+
+            lax.fori_loop(0 if sum(hops) else 1, 2 ** (1 + len(ones)), go, 0, unroll=True)
+
     def send_all(src, dst, sems):
-        def go(i, _):
-            d = lax.rem(me + i, N)
+        def visit(row, col):
             pltpu.make_async_remote_copy(
-                src(d), dst, sems.at[0], sems.at[1], device_id=(d // COLS, lax.rem(d, COLS)), device_id_type=MESH
+                src(row * COLS + col), dst, sems.at[0], sems.at[1], device_id=(row, col), device_id_type=MESH
             ).start()
-            return 0
-
-        lax.fori_loop(1, N, go, 0)
+
+        for_all(visit)
+
+    def greet(row, col):
+        pl.semaphore_signal(barrier, inc=1, device_id=(row, col), device_id_type=MESH)
+
+    for_all(greet)
 
     def send_cols(src, dst, sems):
-        def go(i, _):
-            d = lax.rem(c + i, COLS)
+        def go(t, _):
+            d = column(t)
             pltpu.make_async_remote_copy(
                 src(d), dst, sems.at[0], sems.at[1], device_id=(r, d), device_id_type=MESH
             ).start()
             return 0
 
-        lax.fori_loop(1, COLS, go, 0)
+        lax.fori_loop(0, COLS - 1, go, 0)
 
     def waiter(view, sems):
         return pltpu.make_async_remote_copy(view, view, sems.at[0], sems.at[1], device_id=(r, c), device_id_type=MESH)
 
-    for load in loads[:2]:
+    for load in loads[:3]:
         load.wait()
     pair_flat = pair_ref.reshape(POS, C)
     u = jnp.concatenate(
@@ -254,7 +301,8 @@
     scale_t[...] = jnp.broadcast_to(scale, (8, POS))
     gain = jnp.broadcast_to(gain_first[...], (C, C)).T
     w03 = w_first[:, : 4 * C] * jnp.concatenate([gain] * 4, axis=1)
-    w03_s[...] = left3(w03)
+    w03_s[0] = left3(w03[:, : 2 * C])
+    w03_s[1] = left3(w03[:, 2 * C :])
     proj = dot(left3(turn(w03)), right3(xhat))
     pos = lax.broadcasted_iota(jnp.int32, (8, POS), 1)
     in_row = (r * TI + pos % TI) < valid
@@ -272,11 +320,36 @@
     left = mask * sig0 * p1
     right = mask * sig2 * p3
     sa = send_a.reshape(N * 8, C)
+    sb = send_b.reshape(N * 8, C)
     for q in range(4):
         sa[pl.ds(q, C, stride=8)] = left[:, 128 * q : 128 * (q + 1)]
-        sa[pl.ds(4 + q, C, stride=8)] = right[:, 128 * q : 128 * (q + 1)]
-
-    for load in loads[3:6]:
+        sb[pl.ds(q, C, stride=8)] = right[:, 128 * q : 128 * (q + 1)]
+
+
+    def greet_again(i, _):
+        pl.semaphore_signal(sem_in, inc=1, device_id=(lax.rem(r + i, ROWS), c), device_id_type=MESH)
+        return 0
+
+    pl.semaphore_wait(barrier, N - 1)
+    send_all(lambda d: send_b.at[d, pl.ds(0, 4)], recv_b.at[me, pl.ds(0, 4)], b_sems)
+    recv_b[me] = send_b[me]
+    send_all(lambda d: send_a.at[d, pl.ds(0, 4)], recv_a.at[me, pl.ds(0, 4)], a_sems)
+    recv_a[me] = send_a[me]
+
+    pair_view = pair_ref.reshape(OWN, TJ, TJ, C)
+
+    def send_bias(i, _):
+        d = column(2 * i + 1)
+        pltpu.make_async_remote_copy(
+            bias_any, bias_r.at[:, here], bias_sems.at[0], bias_sems.at[1], device_id=(r, d), device_id_type=MESH
+        ).start()
+        return 0
+
+    lax.fori_loop(0, COLS // 2 - 1, send_bias, 0)
+    send_cols(lambda d: pair_view.at[:, d], pair_r.at[:, here], pair_sems)
+    pair_r[:, here] = pair_view[:, c]
+
+    for load in loads[3:5] + loads[6:9]:
         load.wait()
     w4 = w_first[:, 4 * C :] * gain
     w4_s[...] = left3(w4)
@@ -290,46 +363,21 @@
     w2_s[...] = left3(w_sec)
     w2t_s[...] = left3(turn(w_sec))
 
-    pl.semaphore_wait(barrier, COLS - 1 + ROWS - 1)
-
-    def greet_again(i, _):
-        pl.semaphore_signal(sem_in, inc=1, device_id=(lax.rem(r + i, ROWS), c), device_id_type=MESH)
-        return 0
-
-    lax.fori_loop(1, ROWS, greet_again, 0)
-    pl.semaphore_wait(sem_in, ROWS - 1)
-    send_all(lambda d: send_a.at[d], recv_a.at[me], a_sems)
-    recv_a[me] = send_a[me]
-
-    pair_view = pair_ref.reshape(OWN, TJ, TJ, C)
-
-    def send_bias(i, _):
-        d = lax.rem(c + 2 * i, COLS)
-        pltpu.make_async_remote_copy(
-            bias_any, bias_r.at[:, here], bias_sems.at[0], bias_sems.at[1], device_id=(r, d), device_id_type=MESH
-        ).start()
-        return 0
-
-    lax.fori_loop(1, COLS // 2, send_bias, 0)
-    send_cols(lambda d: pair_view.at[:, d], pair_r.at[:, here], pair_sems)
-    pair_r[:, here] = pair_view[:, c]
-
-    waiter(recv_a.at[pl.ds(0, N - 1)], a_sems).wait_recv()
-    ra = recv_a.reshape(N * 8, C)
-    for part, dest in ((0, at_s), (4, bt_s)):
+    def factor(landing, sems, dest):
+        waiter(landing.at[pl.ds(0, N - 1), pl.ds(0, 4)], sems).wait_recv()
+        ra = landing.reshape(N * 8, C)
         for half in range(2):
             for q in range(4):
-                ys = swap_blocks(
-                    [ra[pl.ds((64 * half + 16 * rr) * 8 + part + q, COLS, stride=8)] for rr in range(4)]
-                )
+                ys = swap_blocks([ra[pl.ds((64 * half + 16 * rr) * 8 + q, COLS, stride=8)] for rr in range(4)])
                 for g in range(4):
                     dest[pl.ds((4 * q + g) * COLS, COLS), pl.ds(128 * half, 128)] = ys[g]
-    at = at_s[...]
-    a_parts = split(at.T)
-    at_parts = split(at)
-    at_hi[...], at_lo[...] = at_parts
-    bt_parts = split(bt_s[...])
+        return dest[...]
+
+    bt_parts = split(factor(recv_b, b_sems, bt_s))
     bt_hi[...], bt_lo[...] = bt_parts
+    at = factor(recv_a, a_sems, at_s)
+    a_parts = split(turn(at))
+    at_hi[...], at_lo[...] = split(at)
     x = mm(a_parts, bt_parts)
     sx = send_x.reshape(N * 8, C)
     for l in range(OWN):
@@ -344,7 +392,7 @@
     send_cols(lambda d: cot_view.at[:, d], cot_r.at[:, here], cot_sems)
     half_bias = COLS // 2 - 1
     waiter(bias_r.reshape(HEADS * T, T).at[pl.ds(0, HEADS * TJ * half_bias)], bias_sems).wait_recv()
-    loads[2].wait()
+    loads[5].wait()
     odd = lax.rem(c, 2)
     bias_view = bias_r.reshape(HEADS, COLS // 2, 2, TJ, T)
     pltpu.make_async_remote_copy(
@@ -399,13 +447,11 @@
 
     out_flat = out_r.reshape(OWN * T, C)
     out_flat[...] = turn(z1 + dot(wot_s[...], right3(g2 * o)))
-    for l in range(OWN):
-        send_cols(
-            lambda d: out_r.at[l, pl.ds(pl.multiple_of(d * TJ, TJ), TJ)], out_ref.at[l * TJ + c], out_sems.at[l]
-        )
-        out_ref[l * TJ + c] = out_r[l, here]
-
-    for load in loads[6:]:
+    out_view = out_ref.reshape(OWN, TJ, TJ, C)
+    send_cols(lambda d: out_r.at[:, pl.ds(pl.multiple_of(d * TJ, TJ), TJ)], out_view.at[:, c], out_sems)
+    out_view[:, c] = out_r[:, here]
+
+    for load in loads[9:]:
         load.wait()
     waiter(cot_r.reshape(OWN * T, C).at[pl.ds(0, OWN * TJ * (COLS - 1))], cot_sems).wait_recv()
     cot = turn(cot_r.reshape(OWN * T, C)[...])
@@ -451,11 +497,9 @@
     grad_part = grad_r.reshape(OWN * T, C)
     dp4 = dz1 * m * g1 * (1.0 - g1)
     grad_part[...] = turn(dz1 + norm_back(dot(w4_s[...], right3(dp4)), ph, ps))
-    for l in range(OWN):
-        send_cols(
-            lambda d: grad_r.at[l, pl.ds(pl.multiple_of(d * TJ, TJ), TJ)], grad_t.at[l * TJ + c], grad_sems.at[l]
-        )
-        grad_t[l * TJ + c] = grad_r[l, here]
+    grad_view = grad_t.reshape(OWN, TJ, TJ, C)
+    send_cols(lambda d: grad_r.at[:, pl.ds(pl.multiple_of(d * TJ, TJ), TJ)], grad_view.at[:, c], grad_sems)
+    grad_view[:, c] = grad_r[:, here]
 
     waiter(recv_d.at[pl.ds(0, N - 1), pl.ds(0, 4)], d_sems).wait_recv()
     rd = recv_d.reshape(N * 8, C)
@@ -466,10 +510,9 @@
                     pl.ds(16 * rr * 8 + 2 * l + jh, COLS, stride=8)
                 ]
     dx_parts = split(dx_s[...])
-    d_bt = mm((at_hi[...], at_lo[...]), dx_parts)
-    d_at = mm((bt_hi[...], bt_lo[...]), dx_parts, NT)
-    sg = send_g.reshape(N * 8, C)
-    for part, d_src in ((0, d_at), (4, d_bt)):
+
+    def send_factor(d_src, buffer, landing, sems):
+        sg = buffer.reshape(N * 8, C)
         for half in range(2):
             for q in range(4):
                 ys = swap_blocks(
@@ -479,61 +522,66 @@
                     ]
                 )
                 for rr in range(4):
-                    sg[pl.ds((64 * half + 16 * rr) * 8 + part + q, COLS, stride=8)] = ys[rr]
-    send_all(lambda d: send_g.at[d], recv_g.at[me], g_sems)
-    recv_g[me] = send_g[me]
-
-    waiter(recv_g.at[pl.ds(0, N - 1)], g_sems).wait_recv()
-    rg = recv_g.reshape(N * 8, C)
-    mask = mask_t[0:1]
-    da = jnp.concatenate([rg[pl.ds(q, C, stride=8)] for q in range(4)], axis=1) * mask
-    db = jnp.concatenate([rg[pl.ds(4 + q, C, stride=8)] for q in range(4)], axis=1) * mask
-    sig0 = proj_t[0]
-    sig2 = proj_t[2]
-    dp1 = da * sig0
-    dp3 = db * sig2
-    dp0 = dp1 * proj_t[1] * (1.0 - sig0)
-    dp2 = dp3 * proj_t[3] * (1.0 - sig2)
-    du = dot(w03_s[...], right3(jnp.concatenate([dp0, dp1, dp2, dp3], axis=0)))
+                    sg[pl.ds((64 * half + 16 * rr) * 8 + q, COLS, stride=8)] = ys[rr]
+        send_all(lambda d: buffer.at[d, pl.ds(0, 4)], landing.at[me, pl.ds(0, 4)], sems)
+        landing[me] = buffer[me]
+
+    send_factor(mm((at_hi[...], at_lo[...]), dx_parts), send_gb, recv_gb, gb_sems)
+    send_factor(mm((bt_hi[...], bt_lo[...]), dx_parts, NT), send_ga, recv_ga, ga_sems)
+
+    def factor_back(n, landing, sems):
+        waiter(landing.at[pl.ds(0, N - 1), pl.ds(0, 4)], sems).wait_recv()
+        rg = landing.reshape(N * 8, C)
+        d = jnp.concatenate([rg[pl.ds(q, C, stride=8)] for q in range(4)], axis=1) * mask_t[0:1]
+        gate = proj_t[n]
+        d_value = d * gate
+        d_gate = d_value * proj_t[n + 1] * (1.0 - gate)
+        return dot(w03_s[n // 2], right3(jnp.concatenate([d_gate, d_value], axis=0)))
+
+    du = factor_back(2, recv_gb, gb_sems)
+    du = du + factor_back(0, recv_ga, ga_sems)
     res = turn(norm_back(du, xhat_t[...], scale_t[0:1]))
     grad_flat = grad_ref.reshape(POS, C)
     part_flat = grad_t.reshape(POS, C)
-    for l in range(OWN):
-        waiter(grad_t.at[pl.ds(0, COLS - 1)], grad_sems.at[l]).wait_recv()
+    waiter(grad_t.at[pl.ds(0, OWN * (COLS - 1))], grad_sems).wait_recv()
     for kk in range(TJ):
         grad_flat[pl.ds(kk, TI, stride=TJ)] = res[TI * kk : TI * (kk + 1)] + part_flat[pl.ds(kk, TI, stride=TJ)]
 
-    waiter(recv_a.at[pl.ds(0, N - 1)], a_sems).wait_send()
+    waiter(recv_a.at[pl.ds(0, N - 1), pl.ds(0, 4)], a_sems).wait_send()
+    waiter(recv_b.at[pl.ds(0, N - 1), pl.ds(0, 4)], b_sems).wait_send()
     waiter(pair_r.reshape(OWN * T, C).at[pl.ds(0, OWN * TJ * (COLS - 1))], pair_sems).wait_send()
     waiter(cot_r.reshape(OWN * T, C).at[pl.ds(0, OWN * TJ * (COLS - 1))], cot_sems).wait_send()
     waiter(bias_r.reshape(HEADS * T, T).at[pl.ds(0, HEADS * TJ * half_bias)], bias_sems).wait_send()
     waiter(bias_r.reshape(HEADS * T, T).at[pl.ds(0, HEADS * T // 2)], twin_sems).wait_send()
-    waiter(recv_g.at[pl.ds(0, N - 1)], g_sems).wait_send()
+    waiter(recv_ga.at[pl.ds(0, N - 1), pl.ds(0, 4)], ga_sems).wait_send()
+    waiter(recv_gb.at[pl.ds(0, N - 1), pl.ds(0, 4)], gb_sems).wait_send()
     waiter(recv_x.at[pl.ds(0, N - 1), pl.ds(0, 4)], x_sems).wait_send()
     waiter(recv_d.at[pl.ds(0, N - 1), pl.ds(0, 4)], d_sems).wait_send()
-    for l in range(OWN):
-        waiter(grad_t.at[pl.ds(0, COLS - 1)], grad_sems.at[l]).wait_send()
-        waiter(out_ref.at[pl.ds(0, COLS - 1)], out_sems.at[l]).wait()
+    waiter(grad_t.at[pl.ds(0, OWN * (COLS - 1))], grad_sems).wait_send()
+    waiter(out_ref.at[pl.ds(0, OWN * (COLS - 1))], out_sems).wait()
 
 
 def body(pair, cotangent, tri_bias, valid_length, gain_first, w_first, gain_mid, w_mid, gain_second, w_second, w_att_out):
     vmem = pl.BlockSpec(memory_space=pltpu.VMEM)
     smem = pl.BlockSpec(memory_space=pltpu.SMEM)
-    anywhere = pl.BlockSpec(memory_space=pl.ANY)
-    tile = jax.ShapeDtypeStruct((TI, TJ, C), F32)
+    hbm = pl.BlockSpec(memory_space=pltpu.HBM)
+    tile = pltpu.VMEM((TI, TJ, C), F32)
     message = pltpu.VMEM((N, 8, C), F32)
     weight = pltpu.VMEM((C, 3 * C), BF16)
     rows = pltpu.VMEM((OWN, T, C), F32)
     square = pltpu.VMEM((T, T), F32)
     square_low = pltpu.VMEM((T, T), BF16)
     pair_of = pltpu.SemaphoreType.DMA((2,))
-    pairs_of = pltpu.SemaphoreType.DMA((OWN, 2))
     return pl.pallas_call(
         kernel,
         out_shape=(tile, tile),
-        in_specs=[smem] + [anywhere] * 3 + [vmem, anywhere] * 3 + [anywhere],
+        in_specs=[smem] + [hbm] * 10,
         out_specs=(vmem, vmem),
         scratch_shapes=[
+            message,
+            message,
+            message,
+            message,
             message,
             message,
             message,
@@ -563,7 +611,7 @@
             pltpu.VMEM((OWN, HEADS, T, T), F32),
             pltpu.VMEM((OWN, HEADS, T, T), BF16),
             pltpu.VMEM((OWN, HEADS, T, T), BF16),
-            pltpu.VMEM((C, 12 * C), BF16),
+            pltpu.VMEM((2, C, 6 * C), BF16),
             weight,
             weight,
             weight,
@@ -577,35 +625,45 @@
             pltpu.VMEM((C, C), F32),
             pltpu.VMEM((C, 4 * C), F32),
             pltpu.VMEM((C, C), F32),
+            pltpu.VMEM((1, C), F32),
+            pltpu.VMEM((1, C), F32),
+            pltpu.VMEM((1, C), F32),
             pltpu.SemaphoreType.REGULAR,
-            pltpu.SemaphoreType.DMA((7,)),
-            pair_of,
-            pair_of,
-            pair_of,
-            pair_of,
-            pair_of,
-            pair_of,
-            pair_of,
-            pair_of,
-            pairs_of,
-            pairs_of,
+            pltpu.SemaphoreType.DMA((10,)),
+            pair_of,
+            pair_of,
+            pair_of,
+            pair_of,
+            pair_of,
+            pair_of,
+            pair_of,
+            pair_of,
+            pair_of,
+            pair_of,
+            pair_of,
+            pair_of,
         ],
         compiler_params=pltpu.CompilerParams(
-            collective_id=0, has_side_effects=True, vmem_limit_bytes=60 * 1024 * 1024
+            collective_id=0, has_side_effects=True, vmem_limit_bytes=48 * 1024 * 1024
         ),
         cost_estimate=pl.CostEstimate(flops=2_000_000_000, bytes_accessed=4_000_000, transcendentals=1_000_000),
     )(
         valid_length,
-        pair,
-        cotangent,
-        tri_bias,
-        gain_first.reshape(1, C),
-        w_first,
-        gain_mid.reshape(1, C),
-        w_mid,
-        gain_second.reshape(1, C),
-        w_second,
-        w_att_out,
+        *(
+            pltpu.with_memory_space_constraint(operand, pltpu.HBM)
+            for operand in (
+                pair,
+                cotangent,
+                tri_bias,
+                gain_first.reshape(1, C),
+                w_first,
+                gain_mid.reshape(1, C),
+                w_mid,
+                gain_second.reshape(1, C),
+                w_second,
+                w_att_out,
+            )
+        ),
     )
 
 

time: 64.6 us -> 59.5 us (0.921)
  Pallas kernels: 60.7 us -> 56.6 us
  local copies, waits for them, and re-layouts: 2.42 us -> 1.41 us
    pallas_call x1, Pallas kernels: 60.7 us -> 56.6 us  [body(): pl.pallas_call(kernel, out_shape=(tile, tile), in_specs=[smem] + [hbm] *...]
    unnamed x4 -> x2, local copies, waits for them, and re-layouts: 2.42 us -> 1.41 us
where the time goes in v4:
time: 59.5 us; the launch traced here: 59.3 us
  Pallas kernels  56.6 us (95%)
  local copies, waits for them, and re-layouts  1.41 us (2%)
  between operations  1.29 us (2%)
    pallas_call x1, Pallas kernels, body(): pl.pallas_call(kernel, out_shape=(tile, tile), in_specs=[smem] + [hbm] *...  56.6 us
    unnamed x2, local copies, waits for them, and re-layouts  1.41 us

profile of v4, /device:TPU:1, one launch (start us, length us, event | category | flops | bytes accessed | tf_op | source)
XLA Modules:
  0.0 59.3 jit_solution(10667135818516669178)
XLA Ops:
  1.3 56.6 %shard_map.122 = (f32[32,16,128]{2,1,0:T(8,128)S(1)}, f32[32,16,128]{2,1,0:T(8,128)S(1)}) custom-call(s32[1]{0:T(128)S(6)} %copy.17.valid_ref, f32[32,16,128]{2,1,0:T(8,128)} %pair_any.1, f32[32,16,128]{2,1,0:T(8,128)} %cot_any.1, f32[4,16,256]{2,1,0:T(8,128)} %bias_any.1, f32[1,128]{1,0:T(1,128)} %bitcast.3, f32[128,640]{1,0:T(8,128)} %w_first_any.1, ...), custom_call_target="tpu_custom_call" | custom-call | flops 2000000000 | bytes 4000000 | tf_op jit(solution)/shard_map/pallas_call | solution.py:575
  57.9 0.7 %copy.15 = f32[32,16,128]{2,1,0:T(8,128)} copy(f32[32,16,128]{2,1,0:T(8,128)S(1)} %get-tuple-element.2) | data formatting | bytes 524288
  58.6 0.7 %copy.16 = f32[32,16,128]{2,1,0:T(8,128)} copy(f32[32,16,128]{2,1,0:T(8,128)S(1)} %get-tuple-element.3) | data formatting | bytes 524288

commit v5 on v4

--- a/solution.py
+++ b/solution.py
@@ -11,6 +11,7 @@
 EPSILON = 1e-05
 MASK_SHIFT = 1000000000.0
 MESH = pl.DeviceIdType.MESH
+LOGICAL = pl.DeviceIdType.LOGICAL
 F32 = jnp.float32
 BF16 = jnp.bfloat16
 NN = (((1,), (0,)), ((), ()))
@@ -173,7 +174,6 @@
     gain_first,
     gain_mid,
     gain_second,
-    sem_in,
     load_sems,
     a_sems,
     b_sems,
@@ -194,23 +194,6 @@
     valid = valid_ref[0]
 
     barrier = pltpu.get_barrier_semaphore()
-
-    def column(t):
-        near = lax.div(t, 8)
-        step = lax.div(lax.rem(t, 8), 2)
-        z = lax.rem(lax.div(c, 4) + 2 + 3 * step + 3 * lax.div(step * (step - 1), 2), 4)
-        hi = lax.rem(lax.div(c, 2) + 1 - near, 2)
-        core = lax.rem(c + 1 - lax.rem(t, 2), 2)
-        return 4 * z + 2 * hi + core
-
-    def greet_col(t, _):
-        pl.semaphore_signal(barrier, inc=1, device_id=(r, column(t)), device_id_type=MESH)
-        return 0
-
-    def greet_row(i, _):
-        pl.semaphore_signal(barrier, inc=1, device_id=(lax.rem(r + i, ROWS), c), device_id_type=MESH)
-        return 0
-
 
     here = pl.ds(pl.multiple_of(c * TJ, TJ), TJ)
     cot_view = cot_any.reshape(OWN, TJ, TJ, C)
@@ -236,10 +219,13 @@
 
     x_at = lax.rem(lax.div(c, 2), 2) * 2 + lax.div(r, 4)
     xs_at = [lax.rem(x_at + n, 4) for n in range(4)]
-    row_of_x = [4 * lax.rem(v, 2) for v in xs_at]
-    col_of_x = [2 * lax.div(v, 2) for v in xs_at]
-    row_of_y = [lax.rem(lax.rem(r, 4) + n, 4) for n in range(4)]
-    col_of_z = [4 * lax.rem(lax.div(c, 4) + n, 4) for n in range(4)]
+    of_x = [4 * COLS * lax.rem(v, 2) + 2 * lax.div(v, 2) for v in xs_at]
+    of_y = [COLS * lax.rem(lax.rem(r, 4) + n, 4) for n in range(4)]
+    of_z = [4 * lax.rem(lax.div(c, 4) + n, 4) for n in range(4)]
+    own_core = lax.rem(c, 2)
+    other_core = 1 - 2 * own_core
+    own_hi = 2 * lax.rem(lax.div(c, 2), 2)
+    of_hi = [own_hi, 2 - own_hi]
 
     def for_all(visit):
         for hops in sorted(itertools.product(range(3), repeat=3), key=lambda h: -sum(h)):
@@ -252,36 +238,44 @@
                     sign = lax.rem(lax.div(t, 2 ** (1 + ones.index(axis))), 2)
                     return options[1] + sign * (options[3] - options[1])
 
-                row = pick(row_of_x, 0) + pick(row_of_y, 1)
-                core = lax.rem(c + lax.rem(t, 2), 2)
-                col = pick(col_of_x, 0) + pick(col_of_z, 2) + core
-                visit(row, col)
+                core = own_core + lax.rem(t, 2) * other_core
+                visit((pick(of_x, 0) + pick(of_y, 1)) + (pick(of_z, 2) + core))
                 return 0
 
             lax.fori_loop(0 if sum(hops) else 1, 2 ** (1 + len(ones)), go, 0, unroll=True)
 
+    def for_cols(visit, cores=2):
+        for hi, z in ((1, 2), (1, 1), (1, 3), (0, 2), (1, 0), (0, 1), (0, 3), (0, 0)):
+
+            def go(t, _):
+                visit(of_hi[hi] + of_z[z] + (own_core + t * other_core))
+                return 0
+
+            if hi + z:
+                lax.fori_loop(0, cores, go, 0, unroll=True)
+            elif cores == 2:
+                go(1, 0)
+
     def send_all(src, dst, sems):
-        def visit(row, col):
+        def visit(d):
             pltpu.make_async_remote_copy(
-                src(row * COLS + col), dst, sems.at[0], sems.at[1], device_id=(row, col), device_id_type=MESH
+                src(d), dst, sems.at[0], sems.at[1], device_id=d, device_id_type=LOGICAL
             ).start()
 
         for_all(visit)
 
-    def greet(row, col):
-        pl.semaphore_signal(barrier, inc=1, device_id=(row, col), device_id_type=MESH)
+    def send_cols(src, dst, sems, cores=2):
+        def visit(d):
+            pltpu.make_async_remote_copy(
+                src(d), dst, sems.at[0], sems.at[1], device_id=r * COLS + d, device_id_type=LOGICAL
+            ).start()
+
+        for_cols(visit, cores)
+
+    def greet(d):
+        pl.semaphore_signal(barrier, inc=1, device_id=d, device_id_type=LOGICAL)
 
     for_all(greet)
-
-    def send_cols(src, dst, sems):
-        def go(t, _):
-            d = column(t)
-            pltpu.make_async_remote_copy(
-                src(d), dst, sems.at[0], sems.at[1], device_id=(r, d), device_id_type=MESH
-            ).start()
-            return 0
-
-        lax.fori_loop(0, COLS - 1, go, 0)
 
     def waiter(view, sems):
         return pltpu.make_async_remote_copy(view, view, sems.at[0], sems.at[1], device_id=(r, c), device_id_type=MESH)
@@ -326,10 +320,6 @@
         sb[pl.ds(q, C, stride=8)] = right[:, 128 * q : 128 * (q + 1)]
 
 
-    def greet_again(i, _):
-        pl.semaphore_signal(sem_in, inc=1, device_id=(lax.rem(r + i, ROWS), c), device_id_type=MESH)
-        return 0
-
     pl.semaphore_wait(barrier, N - 1)
     send_all(lambda d: send_b.at[d, pl.ds(0, 4)], recv_b.at[me, pl.ds(0, 4)], b_sems)
     recv_b[me] = send_b[me]
@@ -338,14 +328,7 @@
 
     pair_view = pair_ref.reshape(OWN, TJ, TJ, C)
 
-    def send_bias(i, _):
-        d = column(2 * i + 1)
-        pltpu.make_async_remote_copy(
-            bias_any, bias_r.at[:, here], bias_sems.at[0], bias_sems.at[1], device_id=(r, d), device_id_type=MESH
-        ).start()
-        return 0
-
-    lax.fori_loop(0, COLS // 2 - 1, send_bias, 0)
+    send_cols(lambda d: bias_any, bias_r.at[:, here], bias_sems, cores=1)
     send_cols(lambda d: pair_view.at[:, d], pair_r.at[:, here], pair_sems)
     pair_r[:, here] = pair_view[:, c]
 
@@ -428,11 +411,12 @@
     g2 = jax.nn.sigmoid(second[3 * C :])
     ots = [[], []]
     inverses = [[], []]
-    for l in range(OWN):
-        js = slice(T * l, T * (l + 1))
-        keys = head_keys(turn(second[C : 2 * C, js]))
-        for h in range(HEADS):
-            hs = slice(WIDTH * h, WIDTH * (h + 1))
+    all_keys = [head_keys(turn(second[C : 2 * C, T * l : T * (l + 1)])) for l in range(OWN)]
+    for h in range(HEADS):
+        hs = slice(WIDTH * h, WIDTH * (h + 1))
+        for l in range(OWN):
+            js = slice(T * l, T * (l + 1))
+            keys = all_keys[l]
             s = dot(keys[h], head_queries(qt_hi[:, js], qt_lo[:, js], h)) + bias_t[h]
             e = jnp.exp(s - jnp.max(s, axis=0, keepdims=True))
             inverse = 1.0 / jnp.sum(e, axis=0, keepdims=True)
@@ -461,11 +445,12 @@
     dqs = [[], []]
     dks = [[], []]
     dvs = [[], []]
-    for l in range(OWN):
-        js = slice(T * l, T * (l + 1))
-        values = head_keys(turn(second[2 * C : 3 * C, js]))
-        for h in range(HEADS):
-            hs = slice(WIDTH * h, WIDTH * (h + 1))
+    all_values = [head_keys(turn(second[2 * C : 3 * C, T * l : T * (l + 1)])) for l in range(OWN)]
+    for h in range(HEADS):
+        hs = slice(WIDTH * h, WIDTH * (h + 1))
+        for l in range(OWN):
+            js = slice(T * l, T * (l + 1))
+            values = all_values[l]
             part = d_o[hs, js] * inverses[l][h]
             delta = jnp.sum(part * ots[l][h], axis=0, keepdims=True)
             dt_hi, dt_lo = split(part)
@@ -561,6 +546,17 @@
     waiter(out_ref.at[pl.ds(0, OWN * (COLS - 1))], out_sems).wait()
 
 
+def store(out_ref, grad_ref, out_any, grad_any, sems):
+    copies = [
+        pltpu.make_async_copy(out_ref, out_any, sems.at[0]),
+        pltpu.make_async_copy(grad_ref, grad_any, sems.at[1]),
+    ]
+    for copy in copies:
+        copy.start()
+    for copy in copies:
+        copy.wait()
+
+
 def body(pair, cotangent, tri_bias, valid_length, gain_first, w_first, gain_mid, w_mid, gain_second, w_second, w_att_out):
     vmem = pl.BlockSpec(memory_space=pltpu.VMEM)
     smem = pl.BlockSpec(memory_space=pltpu.SMEM)
@@ -572,7 +568,7 @@
     square = pltpu.VMEM((T, T), F32)
     square_low = pltpu.VMEM((T, T), BF16)
     pair_of = pltpu.SemaphoreType.DMA((2,))
-    return pl.pallas_call(
+    results = pl.pallas_call(
         kernel,
         out_shape=(tile, tile),
         in_specs=[smem] + [hbm] * 10,
@@ -628,7 +624,6 @@
             pltpu.VMEM((1, C), F32),
             pltpu.VMEM((1, C), F32),
             pltpu.VMEM((1, C), F32),
-            pltpu.SemaphoreType.REGULAR,
             pltpu.SemaphoreType.DMA((10,)),
             pair_of,
             pair_of,
@@ -665,6 +660,16 @@
             )
         ),
     )
+    whole = jax.ShapeDtypeStruct((TI, TJ, C), F32)
+    anywhere = pl.BlockSpec(memory_space=pl.ANY)
+    return pl.pallas_call(
+        store,
+        out_shape=(whole, whole),
+        in_specs=[anywhere, anywhere],
+        out_specs=(anywhere, anywhere),
+        scratch_shapes=[pltpu.SemaphoreType.DMA((2,))],
+        compiler_params=pltpu.CompilerParams(vmem_limit_bytes=16 * 1024 * 1024),
+    )(*(pltpu.with_memory_space_constraint(result, pltpu.VMEM) for result in results))
 
 
 def solution(mesh):

time: 59.5 us -> 58.6 us (0.985)
  local copies, waits for them, and re-layouts: 1.41 us -> 0 us
  Pallas kernels: 56.6 us -> 57.2 us
    unnamed x2 -> x0, local copies, waits for them, and re-layouts: 1.41 us -> none
    pallas_call x0 -> x1, Pallas kernels: none -> 0.81 us  [body(): pl.pallas_call(store, out_shape=(whole, whole), in_specs=[anywhere, anywh...]
where the time goes in v5:
time: 58.6 us; the launch traced here: 58.5 us
  Pallas kernels  57.2 us (98%)
  between operations  1.29 us (2%)
    pallas_call x1, Pallas kernels, body(): pl.pallas_call(kernel, out_shape=(tile, tile), in_specs=[smem] + [hbm] *...  56.4 us

profile of v5, /device:TPU:1, one launch (start us, length us, event | category | flops | bytes accessed | tf_op | source)
XLA Modules:
  0.0 58.5 jit_solution(11118398487127041292)
XLA Ops:
  1.3 56.4 %shard_map.122 = (f32[32,16,128]{2,1,0:T(8,128)S(1)}, f32[32,16,128]{2,1,0:T(8,128)S(1)}) custom-call(s32[1]{0:T(128)S(6)} %copy.13.valid_ref, f32[32,16,128]{2,1,0:T(8,128)} %pair_any.1, f32[32,16,128]{2,1,0:T(8,128)} %cot_any.1, f32[4,16,256]{2,1,0:T(8,128)} %bias_any.1, f32[1,128]{1,0:T(1,128)} %bitcast.3, f32[128,640]{1,0:T(8,128)} %w_first_any.1, ...), custom_call_target="tpu_custom_call" | custom-call | flops 2000000000 | bytes 4000000 | tf_op jit(solution)/shard_map/pallas_call | solution.py:571
  57.7 0.8 %shard_map.123 = (f32[32,16,128]{2,1,0:T(8,128)}, f32[32,16,128]{2,1,0:T(8,128)}) custom-call(f32[32,16,128]{2,1,0:T(8,128)S(1)} %get-tuple-element.4.out_ref, f32[32,16,128]{2,1,0:T(8,128)S(1)} %get-tuple-element.5.grad_ref), custom_call_target="tpu_custom_call" | custom-call | tf_op jit(solution)/shard_map/pallas_call | solution.py:665

commit v6 on v5

--- a/solution.py
+++ b/solution.py
@@ -390,12 +390,6 @@
     pair_t = turn(pair_r.reshape(OWN * T, C)[...])
     ph, ps = norm(pair_t)
     g1 = jax.nn.sigmoid(dot(w4t_s[...], right3(ph)))
-    waiter(bias_r.reshape(HEADS * T, T).at[pl.ds(0, HEADS * T // 2)], twin_sems).wait_recv()
-    key = lax.broadcasted_iota(jnp.int32, (T, T), 0)
-    shift = jnp.where(key < valid, 0.0, -MASK_SHIFT).astype(F32)
-    for h in range(HEADS):
-        bias_t[h] = bias_r[h].T + shift
-
     waiter(recv_x.at[pl.ds(0, N - 1), pl.ds(0, 4)], x_sems).wait_recv()
     rx = recv_x.reshape(N * 8, C)
     x = jnp.concatenate([rx[pl.ds(m, C, stride=8)] for m in range(4)], axis=1)
@@ -409,6 +403,12 @@
     kt_hi, kt_lo = split(second[C : 2 * C])
     vt_hi, vt_lo = split(second[2 * C : 3 * C])
     g2 = jax.nn.sigmoid(second[3 * C :])
+    waiter(bias_r.reshape(HEADS * T, T).at[pl.ds(0, HEADS * T // 2)], twin_sems).wait_recv()
+    key = lax.broadcasted_iota(jnp.int32, (T, T), 0)
+    shift = jnp.where(key < valid, 0.0, -MASK_SHIFT).astype(F32)
+    for h in range(HEADS):
+        bias_t[h] = bias_r[h].T + shift
+
     ots = [[], []]
     inverses = [[], []]
     all_keys = [head_keys(turn(second[C : 2 * C, T * l : T * (l + 1)])) for l in range(OWN)]

time: 58.6 us -> 58.5 us (level)
  no operation moved by 1% of the time
where the time goes in v6:
time: 58.5 us; the launch traced here: 58.4 us
  Pallas kernels  57.1 us (98%)
  between operations  1.29 us (2%)
    pallas_call x1, Pallas kernels, body(): pl.pallas_call(kernel, out_shape=(tile, tile), in_specs=[smem] + [hbm] *...  56.3 us

profile of v6, /device:TPU:1, one launch (start us, length us, event | category | flops | bytes accessed | tf_op | source)
XLA Modules:
  0.0 58.4 jit_solution(443922215292061666)
XLA Ops:
  1.3 56.3 %shard_map.122 = (f32[32,16,128]{2,1,0:T(8,128)S(1)}, f32[32,16,128]{2,1,0:T(8,128)S(1)}) custom-call(s32[1]{0:T(128)S(6)} %copy.13.valid_ref, f32[32,16,128]{2,1,0:T(8,128)} %pair_any.1, f32[32,16,128]{2,1,0:T(8,128)} %cot_any.1, f32[4,16,256]{2,1,0:T(8,128)} %bias_any.1, f32[1,128]{1,0:T(1,128)} %bitcast.3, f32[128,640]{1,0:T(8,128)} %w_first_any.1, ...), custom_call_target="tpu_custom_call" | custom-call | flops 2000000000 | bytes 4000000 | tf_op jit(solution)/shard_map/pallas_call | solution.py:571
  57.6 0.8 %shard_map.123 = (f32[32,16,128]{2,1,0:T(8,128)}, f32[32,16,128]{2,1,0:T(8,128)}) custom-call(f32[32,16,128]{2,1,0:T(8,128)S(1)} %get-tuple-element.4.out_ref, f32[32,16,128]{2,1,0:T(8,128)S(1)} %get-tuple-element.5.grad_ref), custom_call_target="tpu_custom_call" | custom-call | tf_op jit(solution)/shard_map/pallas_call | solution.py:665

commit v7 on v6

--- a/solution.py
+++ b/solution.py
@@ -321,10 +321,10 @@
 
 
     pl.semaphore_wait(barrier, N - 1)
+    send_all(lambda d: send_a.at[d, pl.ds(0, 4)], recv_a.at[me, pl.ds(0, 4)], a_sems)
+    recv_a[me] = send_a[me]
     send_all(lambda d: send_b.at[d, pl.ds(0, 4)], recv_b.at[me, pl.ds(0, 4)], b_sems)
     recv_b[me] = send_b[me]
-    send_all(lambda d: send_a.at[d, pl.ds(0, 4)], recv_a.at[me, pl.ds(0, 4)], a_sems)
-    recv_a[me] = send_a[me]
 
     pair_view = pair_ref.reshape(OWN, TJ, TJ, C)
 
@@ -356,11 +356,11 @@
                     dest[pl.ds((4 * q + g) * COLS, COLS), pl.ds(128 * half, 128)] = ys[g]
         return dest[...]
 
-    bt_parts = split(factor(recv_b, b_sems, bt_s))
-    bt_hi[...], bt_lo[...] = bt_parts
     at = factor(recv_a, a_sems, at_s)
     a_parts = split(turn(at))
     at_hi[...], at_lo[...] = split(at)
+    bt_parts = split(factor(recv_b, b_sems, bt_s))
+    bt_hi[...], bt_lo[...] = bt_parts
     x = mm(a_parts, bt_parts)
     sx = send_x.reshape(N * 8, C)
     for l in range(OWN):

time: 58.5 us -> 58.5 us (level)
  no operation moved by 1% of the time
where the time goes in v7:
time: 58.5 us; the launch traced here: 58.4 us
  Pallas kernels  57.1 us (98%)
  between operations  1.29 us (2%)
    pallas_call x1, Pallas kernels, body(): pl.pallas_call(kernel, out_shape=(tile, tile), in_specs=[smem] + [hbm] *...  56.3 us

profile of v7, /device:TPU:1, one launch (start us, length us, event | category | flops | bytes accessed | tf_op | source)
XLA Modules:
  0.0 58.4 jit_solution(14407170875176590053)
XLA Ops:
  1.3 56.3 %shard_map.122 = (f32[32,16,128]{2,1,0:T(8,128)S(1)}, f32[32,16,128]{2,1,0:T(8,128)S(1)}) custom-call(s32[1]{0:T(128)S(6)} %copy.13.valid_ref, f32[32,16,128]{2,1,0:T(8,128)} %pair_any.1, f32[32,16,128]{2,1,0:T(8,128)} %cot_any.1, f32[4,16,256]{2,1,0:T(8,128)} %bias_any.1, f32[1,128]{1,0:T(1,128)} %bitcast.3, f32[128,640]{1,0:T(8,128)} %w_first_any.1, ...), custom_call_target="tpu_custom_call" | custom-call | flops 2000000000 | bytes 4000000 | tf_op jit(solution)/shard_map/pallas_call | solution.py:571
  57.6 0.8 %shard_map.123 = (f32[32,16,128]{2,1,0:T(8,128)}, f32[32,16,128]{2,1,0:T(8,128)}) custom-call(f32[32,16,128]{2,1,0:T(8,128)S(1)} %get-tuple-element.4.out_ref, f32[32,16,128]{2,1,0:T(8,128)S(1)} %get-tuple-element.5.grad_ref), custom_call_target="tpu_custom_call" | custom-call | tf_op jit(solution)/shard_map/pallas_call | solution.py:665
